TPU v7x, 256 devices: a whole 4x4x8 slice. The times are simulated.
256 devices in a mesh: blk: 16 (over z, y_hi), img: 16 (over x, y_lo, core).
Axes of the slice: x: 4, y: 4 (y_hi: 2, y_lo: 2; y = y_hi * 2 + y_lo), z: 8, core: 2. Of those that a mesh axis runs over, the one named last changes fastest.
Arguments:
- features: bfloat16 [16384, 768], P(('blk', 'img')), may hold values from -6 to 6
- proj: bfloat16 [768, 768], replicated, may hold values from -0.21875 to 0.21875
- student_text: bfloat16 [16384, 768], P(('blk', 'img')), may hold values from -6 to 6
- teacher_image: bfloat16 [16384, 1024], P(('blk', 'img')), may hold values from -25 to 25
- teacher_text: bfloat16 [16384, 1024], P(('blk', 'img')), may hold values from -5 to 5
Outputs:
- row_loss: float32 [16384], P(('blk', 'img'))
- loss: float32 [], replicated
- grad_proj: float32 [768, 768], P('img')
All inputs are finite; a program needn't handle non-finite values.
Results may differ from a plain program's by a relative error of at most 0.003.
Values may be sent and summed in bfloat16 or wider, within the bound.
No kernel may reach another device: no remote copies, remote signals or barrier semaphores. Data moves between devices by JAX's collectives and lax.ppermute only.
A program may use at most 64 MiB of HBM per device.

v0:
```python
import jax
import jax.numpy as jnp
from jax import lax
from jax.sharding import PartitionSpec as P

sig_scale = 10.0
sig_bias = -10.0
teacher_gain = 3.0
eps_value = 1e-06


def unit_rows(values):
    norms = jnp.sqrt(jnp.sum(values * values, axis=-1, keepdims=True) + eps_value)
    return (values / norms, norms)


def per_device(features, proj, student_text, teacher_image, teacher_text):
    rows = features.shape[0]
    width = student_text.shape[1]
    span = lax.axis_size("img")
    cycle_size = lax.axis_size("blk")
    place = lax.axis_index("img")
    blk_place = lax.axis_index("blk")
    block = rows * span
    gain = teacher_gain / jnp.sqrt(jnp.float32(teacher_text.shape[1]))
    s_txt, unused = unit_rows(student_text.astype(jnp.float32))
    s_txt_b = s_txt.astype(jnp.bfloat16)
    text_pair = jnp.concatenate([s_txt_b, teacher_text], axis=1)
    pre = jnp.dot(features, proj, preferred_element_type=jnp.float32)
    s_own, n_own = unit_rows(pre)
    image_b, t_image = (
        lax.all_gather(s_own.astype(jnp.bfloat16), "img", axis=0, tiled=True),
        lax.all_gather(teacher_image, "img", axis=0, tiled=True),
    )
    text_all = lax.all_gather(text_pair, "blk", axis=0, tiled=True)
    cosine = jnp.einsum(
        "qd,kd->qk", image_b, text_all[:, :width], preferred_element_type=jnp.float32
    )
    t_logit = gain * jnp.einsum(
        "qd,kd->qk", t_image, text_all[:, width:], preferred_element_type=jnp.float32
    )
    scores = jnp.stack([cosine, t_logit])
    cosine = scores[0]
    t_logit = scores[1]
    s_logit = sig_scale * cosine
    local_max = jnp.max(t_logit, axis=1)
    s_exp = jnp.exp(s_logit)
    t_max = lax.pmax(local_max, "img")
    t_sum, s_sum = lax.psum(
        (jnp.sum(jnp.exp(t_logit - t_max[:, None]), axis=1), jnp.sum(s_exp, axis=1)), "img"
    )
    t_prob = jnp.exp(t_logit - t_max[:, None]) / t_sum[:, None]
    s_prob = s_exp / s_sum[:, None]
    row_ids = jnp.arange(block, dtype=jnp.int32)[:, None]
    col_ids = jnp.arange(cycle_size * rows, dtype=jnp.int32)[None, :]
    positive = (col_ids // rows == blk_place) & (col_ids % rows + place * rows == row_ids)
    sign = jnp.where(positive, jnp.float32(1.0), jnp.float32(-1.0))
    margin = s_logit + sig_bias
    partial_value = jnp.sum(t_prob * (t_logit - s_logit) + jax.nn.softplus(-sign * margin), axis=1)
    d_cos = (
        sig_scale * (s_prob - t_prob) - sig_scale * sign * jax.nn.sigmoid(-sign * margin)
    ).astype(jnp.bfloat16)
    own_terms = lax.psum_scatter(partial_value, "img", scatter_dimension=0, tiled=True)
    first_row = place * rows
    own_max = lax.dynamic_slice_in_dim(t_max, first_row, rows, 0)
    own_tsum = lax.dynamic_slice_in_dim(t_sum, first_row, rows, 0)
    own_ssum = lax.dynamic_slice_in_dim(s_sum, first_row, rows, 0)
    row_loss = own_terms - (own_max + jnp.log(own_tsum)) + jnp.log(own_ssum)
    loss = lax.psum(jnp.sum(row_loss), ("blk", "img")) / (rows * span * cycle_size)
    d_simg = jnp.dot(d_cos, text_all[:, :width], preferred_element_type=jnp.float32)
    d_own = lax.psum_scatter(d_simg, "img", scatter_dimension=0, tiled=True)
    along = jnp.sum(s_own * d_own, axis=1, keepdims=True)
    d_pre = (d_own - s_own * along) / n_own
    grad_part = jnp.dot(features.astype(jnp.float32).T, d_pre, precision=lax.Precision.HIGHEST)
    grad_rows = lax.psum_scatter(grad_part, "img", scatter_dimension=0, tiled=True)
    grad_proj = lax.psum(grad_rows, "blk")
    return (row_loss, loss, grad_proj)


def solution(mesh):
    return jax.shard_map(
        per_device,
        mesh=mesh,
        in_specs=(
            P(("blk", "img"), None),
            P(),
            P(("blk", "img"), None),
            P(("blk", "img"), None),
            P(("blk", "img"), None),
        ),
        out_specs=(P(("blk", "img")), P(), P("img", None)),
        check_vma=False,
    )
```

profile of v0, /device:TPU:2, one launch (start us, length us, event | category | flops | bytes accessed | tf_op | source)
XLA Modules:
  0.0 563.5 jit_solution(11295212857599136445)
XLA Ops:
  8.0 1.0 fusion.18
  9.0 1.0 fusion.19
  10.0 1.6 pad_maximum_fusion
  11.7 1.3 multiply_reduce_fusion.2
  13.0 0.7 fusion.40
  13.9 35.1 %all-gather.6.cloned.1.call-done = bf16[1024,1024]{1,0:T(8,128)(2,1)} async-done(((bf16[64,1024]{1,0:T(8,128)(2,1)}), bf16[1024,1024]{1,0:T(8,128)(2,1)}) %all-gather.6.cloned.1.call-update) | async-done | bytes 2097168 | tf_op jit(solution)/shard_map/all_gather | solution.py:33
  48.9 99.8 %all-gather.4.cloned.1.call-done = bf16[1024,1792]{1,0:T(8,128)(2,1)} async-done(((bf16[64,1792]{1,0:T(8,128)(2,1)}), bf16[1024,1792]{1,0:T(8,128)(2,1)}) %all-gather.4.cloned.1.call-update) | async-done | bytes 3670032 | tf_op jit(solution)/shard_map/all_gather | solution.py:35
  148.7 6.5 %multiply_reduce_fusion = (f32[1024]{0:T(1024)S(1)}, f32[1024,1024]{1,0:T(8,128)}) fusion(bf16[1024,1024]{1,0:T(8,128)(2,1)} %all-gather.6.cloned.1.call-done, bf16[1024,1792]{1,0:T(8,128)(2,1)} %all-gather.4.cloned.1.call-done), kind=kOutput, calls=%fused_computation.18 | convolution fusion | flops 2149579776 | bytes 8392704 | tf_op jit(solution)/shard_map/qd,kd->qk/dot_general | solution.py:39
  155.2 22.5 %pmax.7 = f32[1024]{0:T(1024)S(1)} all-reduce(f32[1024]{0:T(1024)S(1)} %get-tuple-element.17), channel_id=1, replica_groups=mesh['blk'=16,'img'=16] {'img'}, use_global_device_ids=true, to_apply=%region_2.0 | all-reduce | flops 1024 | bytes 8192 | tf_op jit(solution)/shard_map/pmax | solution.py:48
  177.7 3.0 fusion.10
  180.6 25.4 %psum.28 = f32[1024]{0:T(1024)S(1)} all-reduce(f32[1024]{0:T(1024)S(1)} %fusion.10), channel_id=1, replica_groups=mesh['blk'=16,'img'=16] {'img'}, use_global_device_ids=true, to_apply=%region_4.0 | all-reduce | flops 1024 | bytes 8192 | tf_op jit(solution)/shard_map/psum | solution.py:49
  206.1 10.3 %exponential_reduce_fusion = (f32[1024]{0:T(1024)S(1)}, f32[1024]{0:T(1024)S(1)}, f32[1024,1024]{0,1:T(8,128)}) fusion(s32[1024]{0:T(1024)S(1)} %fusion.32, pred[1024]{0:T(1024)(128)(4,1)S(1)} %fusion.31, f32[1024]{0:T(1024)S(1)} %psum.28, f32[1024]{0:T(1024)S(1)} %pmax.7, f32[1024,1024]{1,0:T(8,128)} %get-tuple-element.18, ...), kind=kOutput, calls=%fused_computation.15 | convolution fusion | flops 1632630784 | bytes 11555840 | tf_op jit(solution)/shard_map/qd,kd->qk/dot_general | solution.py:36
  216.4 27.7 %all-reduce.1 = (f32[1024]{0:T(1024)S(1)}, f32[1024]{0:T(1024)S(1)}) all-reduce(f32[1024]{0:T(1024)S(1)} %get-tuple-element.10, f32[1024]{0:T(1024)S(1)} %get-tuple-element.9), channel_id=2, replica_groups=mesh['blk'=16,'img'=16] {'img'}, use_global_device_ids=true, to_apply=%region_7.0.clone | all-reduce | flops 2048 | bytes 16384
  244.1 10.4 %fusion.13 = f32[1024,768]{1,0:T(8,128)} fusion(f32[1024,1024]{0,1:T(8,128)} %get-tuple-element.19, f32[1024,1024]{1,0:T(8,128)} %get-tuple-element.18, f32[1024]{0:T(1024)S(1)} %get-tuple-element.12, s32[1024]{0:T(1024)S(1)} %fusion.32, f32[1024]{0:T(1024)S(1)} %psum.28, f32[1024]{0:T(1024)S(1)} %pmax.7, pred[1024]{0:T(1024)(128)(4,1)S(1)} %fusion.31, ...), kind=kOutput, calls=%fused_computation.21 | convolution fusion | flops 1631584256 | bytes 13124608 | tf_op jit(solution)/shard_map/dot_general | solution.py:70
  254.6 62.7 %reduce-scatter.5.cloned.1.call-done = f32[64,768]{1,0:T(8,128)} async-done(((f32[1024,768]{1,0:T(8,128)}), f32[64,768]{1,0:T(8,128)}) %reduce-scatter.5.cloned.1.call-update) | async-done | bytes 196624 | tf_op jit(solution)/shard_map/reduce_scatter | solution.py:71
  317.4 1.1 multiply_reduce_fusion.1
  318.5 2.3 convolution_bitcast_fusion
  320.8 2.0 copy.10
  322.9 65.0 %reduce-scatter.7.cloned.1.call-done = f32[48,768]{1,0:T(8,128)} async-done(((f32[768,768]{1,0:T(8,128)}), f32[48,768]{1,0:T(8,128)}) %reduce-scatter.7.cloned.1.call-update) | async-done | bytes 147472
  387.9 1.8 copy.11
  390.9 1.9 fusion.41
  392.8 81.2 %psum.30 = f32[]{:T(128)} all-reduce(f32[]{:T(128)} %get-tuple-element.13), channel_id=1, replica_groups=mesh['blk'=16,'img'=16] {'blk','img'}, use_global_device_ids=true, to_apply=%region_11.12 | all-reduce | flops 1 | bytes 8 | tf_op jit(solution)/shard_map/psum | solution.py:69
  474.7 79.0 %all-reduce.4.cloned.1.call-done = f32[48,768]{0,1:T(8,128)} async-done(((f32[48,768]{0,1:T(8,128)}), f32[48,768]{0,1:T(8,128)}) %all-reduce.4.cloned.1.call-update) | async-done | bytes 147472 | tf_op jit(solution)/shard_map/psum | solution.py:76
  553.7 1.8 copy.9
  (26 shorter events, 1.7 us)
Async XLA Ops:
  7.2 4.5 copy-start
  7.2 41.8 %all-gather.6.cloned.1.call-start = ((), (), s32[]{:S(2)}) async-start(), calls=%async_computation.3 | async-start | bytes 2228224 | tf_op jit(solution)/shard_map/all_gather | solution.py:33
  7.9 140.8 %all-gather.4.cloned.1.call-start = ((), (), s32[]{:S(2)}) async-start(), calls=%async_computation.2 | async-start | bytes 3899392 | tf_op jit(solution)/shard_map/all_gather | solution.py:35
  11.6 194.5 %all-gather.8.cloned.1.call-start = ((), (), s32[]{:S(2)}) async-start(), calls=%async_computation.4 | async-start | bytes 1671168 | tf_op jit(solution)/shard_map/all_gather | solution.py:32
  13.0 304.3 %copy-start.1 = (f32[64,768]{1,0:T(8,128)}, f32[64,768]{1,0:T(8,128)S(1)}, u32[]{:S(2)}) copy-start(f32[64,768]{1,0:T(8,128)S(1)} %get-tuple-element.16) | copy-start | bytes 589828
  13.8 303.6 %reduce-scatter.5.cloned.1.call-start = ((), (), s32[]{:S(2)}) async-start(), calls=%async_computation.5 | async-start | bytes 3342336 | tf_op jit(solution)/shard_map/reduce_scatter | solution.py:71
  244.1 10.5 %copy-start.2 = (f32[1024]{0:T(1024)}, f32[1024]{0:T(1024)S(1)}, u32[]{:S(2)}) copy-start(f32[1024]{0:T(1024)S(1)} %get-tuple-element.12) | copy-start | bytes 12292
  254.6 133.3 %reduce-scatter.7.cloned.1.call-start = ((), (), s32[]{:S(2)}) async-start(), calls=%async_computation.7 | async-start | bytes 2506752
  320.8 68.9 %copy-start.3 = (u32[256]{0:T(256)S(1)}, u32[256]{0:T(256)}, u32[]{:S(2)}) copy-start(u32[256]{0:T(256)} %constant.69) | copy-start | bytes 3076
  322.8 230.9 %all-reduce.4.cloned.1.call-start = ((), (), s32[]{:S(2)}) async-start(), calls=%async_computation.6 | async-start | bytes 786432 | tf_op jit(solution)/shard_map/psum | solution.py:76
Sparse Core Ops, SparseCore 0:
  9.9 39.0 all-gather.5
  51.5 97.1 all-gather.3
  151.1 31.9 all-gather.7
  254.7 62.6 reduce-scatter.4
  322.9 64.8 reduce-scatter.6
  390.3 163.3 all-reduce.3
where the time goes:
time: 564 us; the launch traced here: 563 us
  waiting for transfers between devices  342 us (61%)
  blocking collectives  157 us (28%)
  matrix products  30.9 us (5%)
  between operations  16.7 us (3%)
  other arithmetic  10.4 us (2%)
  local copies, waits for them, and re-layouts  6.21 us (1%)
    all_gather x1, waiting for transfers between devices, per_device(): text_all = lax.all_gather(text_pair, 'blk', axis=0, tiled=True)  99.8 us
    psum x1, blocking collectives, per_device(): lax.psum(jnp.sum(row_loss), ('blk', 'img')) / (rows * span * cycle_size)  81.2 us
    psum x1, waiting for transfers between devices, per_device(): grad_proj = lax.psum(grad_rows, 'blk')  79 us
    unnamed x7, waiting for transfers between devices  65.8 us
    reduce_scatter x1, waiting for transfers between devices, per_device(): d_own = lax.psum_scatter(d_simg, 'img', scatter_dimension=0, tiled=True)  62.7 us
    all_gather x1, waiting for transfers between devices, per_device(): lax.all_gather(teacher_image, 'img', axis=0, tiled=True)  35.1 us
    unnamed x1, blocking collectives  27.7 us
    psum x1, blocking collectives, per_device(): lax.psum((jnp.sum(jnp.exp(t_logit - t_max[:, None]), axis=1), jnp.sum(s_e...  25.4 us
  transfers between devices with their start and end apart: 6, of which 5 were waited for; matrix products, arithmetic and copies ran while one was open for 3% of the time, Pallas kernels for 0%

commit v1 on v0

v1 whole, which is shorter than its diff:
```python
import functools

import jax
import jax.numpy as jnp
import numpy as np
from jax import lax
from jax.experimental import pallas as pl
from jax.experimental.pallas import tpu as pltpu
from jax.sharding import Mesh, PartitionSpec as P

sig_scale = 10.0
sig_bias = -10.0
teacher_gain = 3.0
eps_value = 1e-06

F32 = jnp.float32
BF16 = jnp.bfloat16
NT = (((1,), (1,)), ((), ()))
ALL = ("z", "yh", "x", "yl", "c")
Y = ("yh", "yl")
VMEM_LIMIT = 56 * 1024 * 1024
COLS = 256
CHUNK = 128


def ring(n, k):
    return [(i, (i + k) % n) for i in range(n)]


def flip(n, k):
    return [(i, i ^ k) for i in range(n)]


def whole(shape):
    return pl.BlockSpec(shape, lambda i: (0,) * len(shape))


def logits_kernel(gain, pair_ref, ttxt_ref, stxt_ref, projt_ref, self_ref,
                  te_ref, se_ref, sig_ref, simg_ref, stats_ref, tl, sl):
    dt = ttxt_ref.shape[1]
    texts = ttxt_ref.shape[0]
    tl[...] = gain * lax.dot_general(ttxt_ref[...], pair_ref[:, :dt], NT, preferred_element_type=F32)
    pre = lax.dot_general(projt_ref[...], pair_ref[:, dt:], NT, preferred_element_type=F32)
    norm = jnp.sqrt(jnp.sum(pre * pre, axis=0, keepdims=True) + eps_value)
    simg = pre / norm
    simg_ref[...] = simg
    sl[...] = sig_scale * jnp.dot(stxt_ref[...], simg.astype(BF16), preferred_element_type=F32)
    t_max = jnp.max(tl[...], axis=0, keepdims=True)
    shrink = float(np.exp(sig_bias))

    def step(k, sums):
        rows = pl.ds(pl.multiple_of(k * CHUNK, CHUNK), CHUNK)
        t = tl[rows, :]
        s = sl[rows, :]
        te = jnp.exp(t - t_max)
        se = jnp.exp(s)
        em = se * shrink
        up = 1.0 + em
        inv = 1.0 / up
        sig = em * inv
        soft = jnp.log(up) + (em - (up - 1.0)) * inv
        te_ref[rows, :] = te.astype(BF16)
        se_ref[rows, :] = se.astype(BF16)
        sig_ref[rows, :] = sig.astype(BF16)
        terms = (te, se, te * (t - s), soft)
        return tuple(a + jnp.sum(v.reshape(CHUNK // 8, 8, v.shape[1]), axis=0) for a, v in zip(sums, terms))

    zero = jnp.zeros((8, tl.shape[1]), F32)
    sums = lax.fori_loop(0, texts // CHUNK, step, (zero,) * 4)
    rows = [t_max] + [jnp.sum(v, axis=0, keepdims=True) for v in sums] + [norm]
    rows[4] = rows[4] + self_ref[...]
    stats_ref[...] = jnp.concatenate(rows + [jnp.zeros((2, tl.shape[1]), F32)], axis=0)


def embed_kernel(te_ref, se_ref, sig_ref, simg_ref, stats_ref, txtt_ref, pair_ref, a_ref, b_ref, c_ref, ft_ref):
    simg = simg_ref[...]
    inv = 1.0 / stats_ref[5:6, :]
    for src, dst in ((se_ref, a_ref), (te_ref, b_ref), (sig_ref, c_ref)):
        d = jnp.dot(txtt_ref[...], src[...], preferred_element_type=F32)
        along = jnp.sum(simg * d, axis=0, keepdims=True)
        dst[...] = (d - simg * along) * inv
    width = pair_ref.shape[1] - ft_ref.shape[0]
    ft_ref[...] = pair_ref[:, width:].T


def away_kernel(coef_ref, a_ref, b_ref, c_ref, ft_ref, diag_ref, d_ref, out_ref, acc):
    d = coef_ref[0:1, :] * a_ref[...] + coef_ref[1:2, :] * b_ref[...] + sig_scale * c_ref[...]
    d = d.astype(BF16)
    d_ref[...] = d

    @pl.when(pl.program_id(0) == 0)
    def _():
        acc[...] = diag_ref[...]

    acc[...] += lax.dot_general(ft_ref[...], d, NT, preferred_element_type=F32)

    @pl.when(pl.program_id(0) == pl.num_programs(0) - 1)
    def _():
        out_ref[...] = acc[...].astype(BF16)


def home_kernel(ft_ref, d_ref, diag_ref, out_ref):
    out_ref[...] = diag_ref[...] + lax.dot_general(ft_ref[...], d_ref[...], NT, preferred_element_type=F32)


def params():
    return pltpu.CompilerParams(vmem_limit_bytes=VMEM_LIMIT)


def merge(parts):
    top = functools.reduce(jnp.maximum, [p[0] for p in parts])
    tsum = 0.0
    ssum = 0.0
    tval = 0.0
    soft = 0.0
    for p in parts:
        w = jnp.exp(p[0] - top)
        tsum = tsum + w * p[1]
        ssum = ssum + p[2]
        tval = tval + w * p[3]
        soft = soft + p[4]
    return jnp.stack([top, tsum, ssum, tval, soft])


def per_device(features, proj, student_text, teacher_image, teacher_text):
    rows, feat = features.shape
    dt = teacher_text.shape[1]
    ds = student_text.shape[1]
    zi, yi, xi, ci = lax.axis_index("z"), lax.axis_index(Y), lax.axis_index("x"), lax.axis_index("c")
    yl = lax.axis_index("yl")
    zn, yn, xn = lax.axis_size("z"), lax.axis_size(Y), lax.axis_size("x")
    ylno = lax.axis_size("yl")
    batch = rows * zn * yn * xn * 2
    images = rows * yn * xn
    texts = rows * zn * 2
    gain = float(teacher_gain / np.sqrt(np.float32(dt)))
    cut = feat // (xn * ylno * 2)
    half = feat // 2

    ttxt = lax.all_gather(teacher_text, ("z", "c"), axis=0, tiled=True)
    st = student_text.astype(F32)
    st_own = (st / jnp.sqrt(jnp.sum(st * st, axis=-1, keepdims=True) + eps_value)).astype(BF16)
    stxt = lax.all_gather(st_own, ("z", "c"), axis=0, tiled=True)

    def by_core(v, axis):
        shape = v.shape[:axis] + (feat // (2 * cut), 2, cut) + v.shape[axis + 1:]
        v = v.reshape(shape)
        mine = lax.dynamic_index_in_dim(v, ci, axis + 1, keepdims=False)
        other = lax.dynamic_index_in_dim(v, 1 - ci, axis + 1, keepdims=False)
        out = jnp.concatenate([mine, other], axis=axis)
        return out.reshape(v.shape[:axis] + (feat,) + v.shape[axis + 3:])

    feats = by_core(features, 1)
    projt = by_core(proj, 0).T
    pair = jnp.concatenate([teacher_image, feats], axis=1)
    width = dt + feat

    column = jnp.zeros((yn, rows, width), BF16)
    got = [pair] + [lax.ppermute(pair, Y, ring(yn, k)) for k in (1, 3)]
    got.append(lax.ppermute(got[1], Y, ring(yn, 1)))
    for piece, back in zip(got, (0, 1, 3, 2)):
        column = lax.dynamic_update_slice(column, piece[None], (lax.rem(yi - back + yn, yn), 0, 0))
    column = column.reshape(yn * rows, width)
    from_left = lax.ppermute(column, "x", ring(xn, 1))
    from_right = lax.ppermute(column, "x", ring(xn, 3))
    mid = yn * rows // 2
    far_a = lax.ppermute(from_left[:mid], "x", ring(xn, 1))
    far_b = lax.ppermute(from_right[mid:], "x", ring(xn, 3))
    pairs = jnp.zeros((xn, yn * rows, width), BF16)
    for piece, back, start in ((column, 0, 0), (from_left, 1, 0), (from_right, 3, 0), (far_a, 2, 0), (far_b, 2, mid)):
        pairs = lax.dynamic_update_slice(pairs, piece[None], (lax.rem(xi - back + xn, xn), start, 0))
    pairs = pairs.reshape(images, width)

    pre = jnp.dot(feats, projt.T, preferred_element_type=F32)
    n_own = jnp.sqrt(jnp.sum(pre * pre, axis=-1, keepdims=True) + eps_value)
    s_own = pre / n_own
    s_diag = sig_scale * jnp.sum(s_own.astype(BF16).astype(F32) * st_own.astype(F32), axis=-1)
    self_row = lax.dynamic_update_slice(jnp.zeros((1, images), F32), -(s_diag + sig_bias)[None], (0, (xi * yn + yi) * rows))
    d_diag = -sig_scale * st_own.astype(F32)
    d_diag = (d_diag - s_own * jnp.sum(s_own * d_diag, axis=1, keepdims=True)) / n_own
    g_diag = jnp.dot(feats.astype(F32).T, d_diag, precision=lax.Precision.HIGHEST)

    blocks = images // COLS
    col = lambda n: pl.BlockSpec((n, COLS), lambda i: (0, i))
    te, se, sig, simg, stats = pl.pallas_call(
        functools.partial(logits_kernel, gain),
        grid=(blocks,),
        in_specs=[pl.BlockSpec((COLS, width), lambda i: (i, 0)), whole((texts, dt)), whole((texts, ds)), whole((ds, feat)), col(1)],
        out_specs=[col(texts), col(texts), col(texts), col(ds), col(8)],
        out_shape=[jax.ShapeDtypeStruct((texts, images), BF16)] * 3
        + [jax.ShapeDtypeStruct((ds, images), F32), jax.ShapeDtypeStruct((8, images), F32)],
        scratch_shapes=[pltpu.VMEM((texts, COLS), F32), pltpu.VMEM((texts, COLS), F32)],
        compiler_params=params(),
        cost_estimate=pl.CostEstimate(flops=2 * images * (texts * (dt + ds) + feat * ds), bytes_accessed=20 << 20, transcendentals=4 * images * texts),
        name="logits",
    )(pairs, ttxt, stxt, projt, self_row)

    a, b, c, ft = pl.pallas_call(
        embed_kernel,
        grid=(blocks,),
        in_specs=[col(texts), col(texts), col(texts), col(ds), col(8), whole((ds, texts)), pl.BlockSpec((COLS, width), lambda i: (i, 0))],
        out_specs=[col(ds), col(ds), col(ds), col(feat)],
        out_shape=[jax.ShapeDtypeStruct((ds, images), F32)] * 3 + [jax.ShapeDtypeStruct((feat, images), BF16)],
        compiler_params=params(),
        cost_estimate=pl.CostEstimate(flops=6 * images * texts * ds, bytes_accessed=20 << 20, transcendentals=0),
        name="embed",
    )(te, se, sig, simg, stats, stxt.T, pairs)

    own = stats[:5]
    own = merge([own] + [lax.ppermute(own, Y, ring(yn, k)) for k in (1, 3, 2)])
    own = merge([own] + [lax.ppermute(own, "x", ring(xn, k)) for k in (1, 3, 2)])
    t_max, t_sum, s_sum, t_val, soft = own
    coef = jnp.stack([sig_scale / s_sum, -sig_scale * jnp.exp(stats[0] - t_max) / t_sum])

    d, away = pl.pallas_call(
        away_kernel,
        grid=(blocks,),
        in_specs=[col(2), col(ds), col(ds), col(ds), pl.BlockSpec((half, COLS), lambda i: (1, i)), pl.BlockSpec((half, ds), lambda i: (1, 0))],
        out_specs=[col(ds), whole((half, ds))],
        out_shape=[jax.ShapeDtypeStruct((ds, images), BF16), jax.ShapeDtypeStruct((half, ds), BF16)],
        scratch_shapes=[pltpu.VMEM((half, ds), F32)],
        compiler_params=params(),
        name="away",
    )(coef, a, b, c, ft, g_diag)
    arrived = lax.ppermute(away, "c", flip(2, 1))
    home = pl.pallas_call(
        home_kernel,
        grid=(1,),
        in_specs=[pl.BlockSpec((half, images), lambda i: (0, 0)), whole((ds, images)), pl.BlockSpec((half, ds), lambda i: (0, 0))],
        out_specs=whole((half, ds)),
        out_shape=jax.ShapeDtypeStruct((half, ds), F32),
        compiler_params=params(),
        cost_estimate=pl.CostEstimate(flops=2 * images * half * ds, bytes_accessed=6 << 20, transcendentals=0),
        name="home",
    )(ft, d, g_diag)

    value = t_val / t_sum + soft - (t_max + jnp.log(t_sum)) + jnp.log(s_sum)
    row_loss = lax.dynamic_slice_in_dim(value, (xi * yn + yi) * rows, rows, 0)
    loss_row = jnp.full((8, 128), jnp.sum(value), F32)
    loss_row = loss_row + lax.ppermute(loss_row, "c", flip(2, 1))

    g = (home + arrived.astype(F32)).reshape(xn, ylno * cut, ds)
    send = lambda k: lax.ppermute(lax.dynamic_index_in_dim(g, lax.rem(xi + k, xn), 0, keepdims=False).astype(BF16), "x", ring(xn, k))
    parts = [send(k) for k in (1, 3, 2)]
    g = lax.dynamic_index_in_dim(g, xi, 0, keepdims=False) + sum(p.astype(F32) for p in parts)
    g = g.reshape(ylno, cut, ds)
    mine = lax.dynamic_index_in_dim(g, yl, 0, keepdims=False)
    other = lax.dynamic_index_in_dim(g, 1 - yl, 0, keepdims=False).astype(BF16)
    parts = [lax.ppermute(other, Y, ring(yn, k)) for k in (1, 3)] + [lax.ppermute(mine.astype(BF16), Y, ring(yn, 2))]
    mine = mine + sum(p.astype(F32) for p in parts)
    tail = jnp.concatenate([mine, jnp.broadcast_to(loss_row[:, :1], (8, ds))], axis=0)
    for k in (1, 2, 4):
        tail = tail + lax.ppermute(tail, "z", flip(zn, k))
    return (row_loss, tail[cut, 0] / batch, tail[:cut])


def solution(mesh):
    sizes = dict(mesh.shape)
    fine = Mesh(np.asarray(mesh.devices).reshape(sizes["blk"] // 2, 2, sizes["img"] // 4, 2, 2), ALL)
    return jax.shard_map(
        per_device,
        mesh=fine,
        in_specs=(P(ALL, None), P(), P(ALL, None), P(ALL, None), P(ALL, None)),
        out_specs=(P(ALL), P(), P(("x", "yl", "c"), None)),
        check_vma=False,
    )
```

time: 564 us -> 212 us (0.38)
  waiting for transfers between devices: 342 us -> 92.4 us
  blocking collectives: 157 us -> 0 us
  Pallas kernels: 0 us -> 42.3 us
  starting transfers between devices: 0.24 us -> 31.5 us
  matrix products: 30.9 us -> 3.04 us
  local copies, waits for them, and re-layouts: 6.21 us -> 20.2 us
    psum x2 -> x0, blocking collectives: 107 us -> none  [the longest x1 81.2 us: per_device(): lax.psum(jnp.sum(row_loss), ('blk', 'img')) / (rows * span * cycle_size)]
    all_gather x3 -> x2, waiting for transfers between devices: 135 us -> 31.2 us  [the longest x1 31.2 us: per_device(): ttxt = lax.all_gather(teacher_text, ('z', 'c'), axis=0, tiled=True)]
    psum x1 -> x0, waiting for transfers between devices: 79 us -> none  [per_device(): grad_proj = lax.psum(grad_rows, 'blk')]
    unnamed x7 -> x2, waiting for transfers between devices: 65.8 us -> 0.04 us
    reduce_scatter x1 -> x0, waiting for transfers between devices: 62.7 us -> none  [per_device(): d_own = lax.psum_scatter(d_simg, 'img', scatter_dimension=0, tiled=True)]
    ppermute x0 -> x24, waiting for transfers between devices: none -> 61.2 us  [the longest x3 21.9 us: per_device(): tail = tail + lax.ppermute(tail, 'z', flip(zn, k))]
    pallas_call x0 -> x4, Pallas kernels: none -> 42.3 us  [the longest x1 18 us: per_device(): pl.pallas_call(functools.partial(logits_kernel, gain), grid=(blocks,), in...]
    ppermute x0 -> x24, starting transfers between devices: none -> 31.4 us  [the longest x3 5.36 us: per_device(): tail = tail + lax.ppermute(tail, 'z', flip(zn, k))]
  transfers between devices with their start and end apart: 6 -> 26, of which waited for: 5 -> 14; matrix products, arithmetic and copies ran while one was open for 3% -> 9% of each run, Pallas kernels for 0% -> 8%
where the time goes in v1:
time: 212 us; the launch traced here: 211 us
  waiting for transfers between devices  92.4 us (44%)
  Pallas kernels  42.3 us (20%)
  starting transfers between devices  31.5 us (15%)
  local copies, waits for them, and re-layouts  20.2 us (10%)
  between operations  16.2 us (8%)
  other arithmetic  5.67 us (3%)
  matrix products  3.04 us (1%)
    all_gather x1, waiting for transfers between devices, per_device(): ttxt = lax.all_gather(teacher_text, ('z', 'c'), axis=0, tiled=True)  31.2 us
    ppermute x3, waiting for transfers between devices, per_device(): tail = tail + lax.ppermute(tail, 'z', flip(zn, k))  21.9 us
    pallas_call x1, Pallas kernels, per_device(): pl.pallas_call(functools.partial(logits_kernel, gain), grid=(blocks,), in...  18 us
    ppermute x1, waiting for transfers between devices, per_device(): from_left = lax.ppermute(column, 'x', ring(xn, 1))  13.7 us
    pallas_call x1, Pallas kernels, per_device(): pl.pallas_call(embed_kernel, grid=(blocks,), in_specs=[col(texts), col(te...  12.8 us
    pallas_call x1, Pallas kernels, per_device(): pl.pallas_call(away_kernel, grid=(blocks,), in_specs=[col(2), col(ds), co...  7.6 us
    ppermute x1, waiting for transfers between devices, per_device(): got.append(lax.ppermute(got[1], Y, ring(yn, 1)))  7.39 us
    dynamic_update_slice x5, local copies, waits for them, and re-layouts, per_device(): lax.dynamic_update_slice(pairs, piece[None], (lax.rem(xi - back + xn, xn)...  6.93 us
  transfers between devices with their start and end apart: 26, of which 14 were waited for; matrix products, arithmetic and copies ran while one was open for 9% of the time, Pallas kernels for 8%

profile of v1, /device:TPU:2, one launch (start us, length us, event | category | flops | bytes accessed | tf_op | source)
XLA Modules:
  0.0 211.3 jit_solution(7039643246580678019)
XLA Ops:
  15.4 5.2 %collective-permute-done = bf16[64,1792]{1,0:T(8,128)(2,1)S(1)} collective-permute-done((bf16[64,1792]{1,0:T(8,128)(2,1)S(1)}, bf16[64,1792]{1,0:T(8,128)(2,1)S(1)}, u32[]{:S(2)}, u32[]{:S(2)}) %collective-permute-start) | collective-permute-done | bytes 229408 | tf_op jit(solution)/shard_map/ppermute | solution.py:159
  21.0 7.4 %collective-permute-done.2 = bf16[64,1792]{1,0:T(8,128)(2,1)S(1)} collective-permute-done((bf16[64,1792]{1,0:T(8,128)(2,1)S(1)}, bf16[64,1792]{1,0:T(8,128)(2,1)S(1)}, u32[]{:S(2)}, u32[]{:S(2)}) %collective-permute-start.2) | collective-permute-done | bytes 229408 | tf_op jit(solution)/shard_map/ppermute | solution.py:160
  35.3 13.7 %collective-permute-done.3 = bf16[256,1792]{1,0:T(8,128)(2,1)} collective-permute-done((bf16[256,1792]{1,0:T(8,128)(2,1)S(1)}, bf16[256,1792]{1,0:T(8,128)(2,1)}, u32[]{:S(2)}, u32[]{:S(2)}) %collective-permute-start.3) | collective-permute-done | bytes 917536 | tf_op jit(solution)/shard_map/ppermute | solution.py:164
  53.3 2.2 %bitcast_dynamic-update-slice_fusion.1 = bf16[4,256,1792]{2,1,0:T(8,128)(2,1)} fusion(bf16[4,256,1792]{2,1,0:T(8,128)(2,1)} %bitcast_dynamic-update-slice_fusion.2, s32[]{:T(128)S(6)} %select_n.60, bf16[256,1792]{1,0:T(8,128)(2,1)} %collective-permute-done.3), kind=kLoop, calls=%fused_computation.4 | loop fusion | bytes 1835012 | tf_op jit(solution)/shard_map/dynamic_update_slice | solution.py:171
  55.5 2.2 %bitcast_dynamic-update-slice_fusion = bf16[4,256,1792]{2,1,0:T(8,128)(2,1)} fusion(bf16[4,256,1792]{2,1,0:T(8,128)(2,1)} %bitcast_dynamic-update-slice_fusion.1, s32[]{:T(128)S(6)} %select_n.61, bf16[256,1792]{1,0:T(8,128)(2,1)} %collective-permute-done.4), kind=kLoop, calls=%fused_computation.3 | loop fusion | bytes 1835012 | tf_op jit(solution)/shard_map/dynamic_update_slice | solution.py:171
  57.6 2.1 collective-permute-done.5
  62.9 31.2 %all-gather.3.cloned.1.call-done.ttxt_ref = bf16[1024,1024]{1,0:T(8,128)(2,1)} async-done(((bf16[64,1024]{1,0:T(8,128)(2,1)}), bf16[1024,1024]{1,0:T(8,128)(2,1)}) %all-gather.3.cloned.1.call-update) | async-done | bytes 2097168 | tf_op jit(solution)/shard_map/all_gather | solution.py:140
  94.1 18.0 %logits.1 = (bf16[1024,1024]{1,0:T(8,128)(2,1)}, bf16[1024,1024]{1,0:T(8,128)(2,1)}, bf16[1024,1024]{1,0:T(8,128)(2,1)}, f32[768,1024]{1,0:T(8,128)}, f32[8,1024]{1,0:T(8,128)}) custom-call(bf16[1024,1792]{1,0:T(8,128)(2,1)} %bitcast.13.pair_ref, bf16[1024,1024]{1,0:T(8,128)(2,1)} %all-gather.3.cloned.1.call-done.ttxt_ref, ...), custom_call_target="tpu_custom_call" | custom-call | flops 4966055936 | bytes 20971520 | tf_op jit(solution)/shard_map/logits/pallas_call | solution.py:185
  112.1 3.1 %collective-permute-start.9 = (f32[5,1024]{1,0:T(8,128)}, f32[5,1024]{1,0:T(8,128)S(1)}, u32[]{:S(2)}, u32[]{:S(2)}) collective-permute-start(f32[5,1024]{1,0:T(8,128)} %bitcast.100), channel_id=1, source_target_pairs={{0,16},{2,18},{16,0},{18,2},{1,17},{3,19},{17,1},{19,3},{4,20},{6,... | collective-permute-start | bytes 61448 | tf_op jit(solution)/shard_map/ppermute | solution.py:210
  117.2 2.6 %fusion.4.diag_ref = f32[768,768]{1,0:T(8,128)} fusion(bf16[64,768]{0,1:T(8,128)(2,1)S(1)} %bitcast.90, bf16[64,768]{1,0:T(8,128)(2,1)S(1)} %copy-done.2, f32[64]{0:T(128)S(1)} %get-tuple-element.25, f32[64]{0:T(128)S(1)} %get-tuple-element.70, f32[64,768]{1,0:T(8,128)S(1)} %copy-done.4), kind=kOutput, calls=%fused_computation.27 | convolution fusion | flops 453279744 | bytes 2753024 | tf_op jit(solution)/shard_map/dot_general | solution.py:181
  121.8 2.2 %collective-permute-start.12 = (f32[5,1024]{1,0:T(8,128)S(1)}, f32[5,1024]{1,0:T(8,128)S(1)}, u32[]{:S(2)}, u32[]{:S(2)}) collective-permute-start(f32[5,1024]{1,0:T(8,128)S(1)} %stack.4), channel_id=1, source_target_pairs={{0,8},{4,12},{8,0},{12,4},{1,9},{5,13},{9,1},{13,5},{2,10},{6,14},... | collective-permute-start | bytes 61448 | tf_op jit(solution)/shard_map/ppermute | solution.py:211
  126.0 12.8 %embed.1 = (f32[768,1024]{1,0:T(8,128)}, f32[768,1024]{1,0:T(8,128)}, f32[768,1024]{1,0:T(8,128)}, bf16[768,1024]{1,0:T(8,128)(2,1)}) custom-call(bf16[1024,1024]{1,0:T(8,128)(2,1)} %get-tuple-element.15.te_ref, bf16[1024,1024]{1,0:T(8,128)(2,1)} %get-tuple-element.16.se_ref, bf16[1024,1024]{1,0:T(8,128)(2,1)} %get-tuple-element.17.sig_ref, ...), custom_call_target="tpu_custom_call" | custom-call | flops 4831838208 | bytes 20971520 | tf_op jit(solution)/shard_map/embed/pallas_call | solution.py:198
  140.4 7.6 %away.1 = (bf16[768,1024]{1,0:T(8,128)(2,1)}, bf16[384,768]{1,0:T(8,128)(2,1)}) custom-call(f32[2,1024]{1,0:T(2,128)} %pad_maximum_fusion.4.coef_ref, f32[768,1024]{1,0:T(8,128)} %get-tuple-element.20.a_ref, f32[768,1024]{1,0:T(8,128)} %get-tuple-element.21.b_ref, f32[768,1024]{1,0:T(8,128)} %get-tuple-element.22.c_ref, ...), custom_call_target="tpu_custom_call" | custom-call | tf_op jit(solution)/shard_map/away/pallas_call | solution.py:215
  148.0 3.8 %home.1 = f32[384,768]{1,0:T(8,128)} custom-call(bf16[768,1024]{1,0:T(8,128)(2,1)} %get-tuple-element.19.ft_ref, bf16[768,1024]{1,0:T(8,128)(2,1)} %get-tuple-element.23.d_ref, f32[768,768]{1,0:T(8,128)} %fusion.4.diag_ref), custom_call_target="tpu_custom_call" | custom-call | flops 603979776 | bytes 6291456 | tf_op jit(solution)/shard_map/home/pallas_call | solution.py:226
  153.3 2.8 %collective-permute-start.16 = (bf16[96,768]{1,0:T(8,128)(2,1)S(1)}, bf16[96,768]{1,0:T(8,128)(2,1)S(1)}, u32[]{:S(2)}, u32[]{:S(2)}) collective-permute-start(bf16[96,768]{1,0:T(8,128)(2,1)S(1)} %get-tuple-element.35), channel_id=1, source_target_pairs={{0,8},{4,12},{8,0},{12,4},{1,9},{5,13},{9,1},{13,5},{2,10},{6,14},... | collective-permute-start | bytes 442376 | tf_op jit(solution)/shard_map/ppermute | solution.py:243
  156.1 2.0 collective-permute-start.14
  159.5 2.1 collective-permute-done.16
  161.6 2.7 %collective-permute-done.15 = bf16[96,768]{1,0:T(8,128)(2,1)S(1)} collective-permute-done((bf16[96,768]{1,0:T(8,128)(2,1)S(1)}, bf16[96,768]{1,0:T(8,128)(2,1)S(1)}, u32[]{:S(2)}, u32[]{:S(2)}) %collective-permute-start.15) | collective-permute-done | bytes 147488 | tf_op jit(solution)/shard_map/ppermute | solution.py:243
  164.4 2.2 %collective-permute-start.18 = (bf16[48,768]{1,0:T(8,128)(2,1)S(1)}, bf16[48,768]{1,0:T(8,128)(2,1)S(1)}, u32[]{:S(2)}, u32[]{:S(2)}) collective-permute-start(bf16[48,768]{1,0:T(8,128)(2,1)S(1)} %get-tuple-element.39), channel_id=1, source_target_pairs={{0,18},{2,0},{16,2},{18,16},{1,19},{3,1},{17,3},{19,17},{4,22},{6,... | collective-permute-start | bytes 221192 | tf_op jit(solution)/shard_map/ppermute | solution.py:249
  169.2 3.4 %collective-permute-done.19 = bf16[48,768]{1,0:T(8,128)(2,1)S(1)} collective-permute-done((bf16[48,768]{1,0:T(8,128)(2,1)S(1)}, bf16[48,768]{1,0:T(8,128)(2,1)S(1)}, u32[]{:S(2)}, u32[]{:S(2)}) %collective-permute-start.19) | collective-permute-done | bytes 73760 | tf_op jit(solution)/shard_map/ppermute | solution.py:249
  174.4 5.0 %collective-permute-done.21 = f32[56,768]{1,0:T(8,128)S(1)} collective-permute-done((f32[56,768]{1,0:T(8,128)S(1)}, f32[56,768]{1,0:T(8,128)S(1)}, u32[]{:S(2)}, u32[]{:S(2)}) %collective-permute-start.21) | collective-permute-done | bytes 172064 | tf_op jit(solution)/shard_map/ppermute | solution.py:253
  181.1 7.9 %collective-permute-done.22 = f32[56,768]{1,0:T(8,128)S(1)} collective-permute-done((f32[56,768]{1,0:T(8,128)S(1)}, f32[56,768]{1,0:T(8,128)S(1)}, u32[]{:S(2)}, u32[]{:S(2)}) %collective-permute-start.22) | collective-permute-done | bytes 172064 | tf_op jit(solution)/shard_map/ppermute | solution.py:253
  189.1 2.8 %collective-permute-start.23 = (f32[56,768]{1,0:T(8,128)S(1)}, f32[56,768]{1,0:T(8,128)S(1)}, u32[]{:S(2)}, u32[]{:S(2)}) collective-permute-start(f32[56,768]{1,0:T(8,128)S(1)} %add.384), channel_id=1, source_target_pairs={{0,128},{32,160},{64,192},{96,224},{128,0},{160,32},{192,64},{224,... | collective-permute-start | bytes 516104 | tf_op jit(solution)/shard_map/ppermute | solution.py:253
  192.5 9.0 %collective-permute-done.23 = f32[56,768]{1,0:T(8,128)S(1)} collective-permute-done((f32[56,768]{1,0:T(8,128)S(1)}, f32[56,768]{1,0:T(8,128)S(1)}, u32[]{:S(2)}, u32[]{:S(2)}) %collective-permute-start.23) | collective-permute-done | bytes 172064 | tf_op jit(solution)/shard_map/ppermute | solution.py:253
  (109 shorter events, 41.0 us)
Async XLA Ops:
  7.2 55.7 %all-gather.5.cloned.1.call-start = ((), (), s32[]{:S(2)}) async-start(), calls=%async_computation.1 | async-start | bytes 1671168 | tf_op jit(solution)/shard_map/all_gather | solution.py:143
  11.7 82.4 %all-gather.3.cloned.1.call-start = ((), (), s32[]{:S(2)}) async-start(), calls=%async_computation | async-start | bytes 2228224 | tf_op jit(solution)/shard_map/all_gather | solution.py:140
  12.0 8.7 %collective-permute-start = (bf16[64,1792]{1,0:T(8,128)(2,1)S(1)}, bf16[64,1792]{1,0:T(8,128)(2,1)S(1)}, u32[]{:S(2)}, u32[]{:S(2)}) collective-permute-start(bf16[64,1792]{1,0:T(8,128)(2,1)S(1)} %pad_maximum_fusion.1), channel_id=1, source_target_pairs={{0,2},{2,16},{16,18},{18,0},{1,3},{3,17},{17,19},{19,1},{4,6},{6,2... | collective-permute-start | bytes 688136 | tf_op jit(solution)/shard_map/ppermute | solution.py:159
  13.6 7.4 %collective-permute-start.1 = (bf16[64,1792]{1,0:T(8,128)(2,1)S(1)}, bf16[64,1792]{1,0:T(8,128)(2,1)S(1)}, u32[]{:S(2)}, u32[]{:S(2)}) collective-permute-start(bf16[64,1792]{1,0:T(8,128)(2,1)S(1)} %pad_maximum_fusion.1), channel_id=1, source_target_pairs={{0,18},{2,0},{16,2},{18,16},{1,19},{3,1},{17,3},{19,17},{4,22},{6,... | collective-permute-start | bytes 688136 | tf_op jit(solution)/shard_map/ppermute | solution.py:159
  20.7 7.8 %collective-permute-start.2 = (bf16[64,1792]{1,0:T(8,128)(2,1)S(1)}, bf16[64,1792]{1,0:T(8,128)(2,1)S(1)}, u32[]{:S(2)}, u32[]{:S(2)}) collective-permute-start(bf16[64,1792]{1,0:T(8,128)(2,1)S(1)} %collective-permute-done), channel_id=1, source_target_pairs={{0,2},{2,16},{16,18},{18,0},{1,3},{3,17},{17,19},{19,1},{4,6},{6,2... | collective-permute-start | bytes 688136 | tf_op jit(solution)/shard_map/ppermute | solution.py:160
  28.4 20.6 %collective-permute-start.3 = (bf16[256,1792]{1,0:T(8,128)(2,1)S(1)}, bf16[256,1792]{1,0:T(8,128)(2,1)}, u32[]{:S(2)}, u32[]{:S(2)}) collective-permute-start(bf16[256,1792]{1,0:T(8,128)(2,1)S(1)} %bitcast.84), channel_id=1, source_target_pairs={{0,4},{4,8},{8,12},{12,0},{1,5},{5,9},{9,13},{13,1},{2,6},{6,10},{... | collective-permute-start | bytes 2752520 | tf_op jit(solution)/shard_map/ppermute | solution.py:164
  30.0 21.6 %collective-permute-start.4 = (bf16[256,1792]{1,0:T(8,128)(2,1)S(1)}, bf16[256,1792]{1,0:T(8,128)(2,1)}, u32[]{:S(2)}, u32[]{:S(2)}) collective-permute-start(bf16[256,1792]{1,0:T(8,128)(2,1)S(1)} %bitcast.85), channel_id=1, source_target_pairs={{0,12},{4,0},{8,4},{12,8},{1,13},{5,1},{9,5},{13,9},{2,14},{6,2},{... | collective-permute-start | bytes 2752520 | tf_op jit(solution)/shard_map/ppermute | solution.py:165
  50.1 9.7 %collective-permute-start.5 = (bf16[128,1792]{1,0:T(8,128)(2,1)S(1)}, bf16[128,1792]{1,0:T(8,128)(2,1)S(1)}, u32[]{:S(2)}, u32[]{:S(2)}) collective-permute-start(bf16[128,1792]{1,0:T(8,128)(2,1)S(1)} %slice.177), channel_id=1, source_target_pairs={{0,4},{4,8},{8,12},{12,0},{1,5},{5,9},{9,13},{13,1},{2,6},{6,10},{... | collective-permute-start | bytes 1376264 | tf_op jit(solution)/shard_map/ppermute | solution.py:167
  52.7 9.4 %collective-permute-start.6 = (bf16[128,1792]{1,0:T(8,128)(2,1)S(1)}, bf16[128,1792]{1,0:T(8,128)(2,1)S(1)}, u32[]{:S(2)}, u32[]{:S(2)}) collective-permute-start(bf16[128,1792]{1,0:T(8,128)(2,1)S(1)} %slice.178), channel_id=1, source_target_pairs={{0,12},{4,0},{8,4},{12,8},{1,13},{5,1},{9,5},{13,9},{2,14},{6,2},{... | collective-permute-start | bytes 1376264 | tf_op jit(solution)/shard_map/ppermute | solution.py:168
  112.1 9.3 %collective-permute-start.9 = (f32[5,1024]{1,0:T(8,128)}, f32[5,1024]{1,0:T(8,128)S(1)}, u32[]{:S(2)}, u32[]{:S(2)}) collective-permute-start(f32[5,1024]{1,0:T(8,128)} %bitcast.100), channel_id=1, source_target_pairs={{0,16},{2,18},{16,0},{18,2},{1,17},{3,19},{17,1},{19,3},{4,20},{6,... | collective-permute-start | bytes 61448 | tf_op jit(solution)/shard_map/ppermute | solution.py:210
  115.2 6.2 %collective-permute-start.8 = (f32[5,1024]{1,0:T(8,128)}, f32[5,1024]{1,0:T(8,128)S(1)}, u32[]{:S(2)}, u32[]{:S(2)}) collective-permute-start(f32[5,1024]{1,0:T(8,128)} %bitcast.101), channel_id=1, source_target_pairs={{0,18},{2,0},{16,2},{18,16},{1,19},{3,1},{17,3},{19,17},{4,22},{6,... | collective-permute-start | bytes 61448 | tf_op jit(solution)/shard_map/ppermute | solution.py:210
  121.8 17.0 %collective-permute-start.12 = (f32[5,1024]{1,0:T(8,128)S(1)}, f32[5,1024]{1,0:T(8,128)S(1)}, u32[]{:S(2)}, u32[]{:S(2)}) collective-permute-start(f32[5,1024]{1,0:T(8,128)S(1)} %stack.4), channel_id=1, source_target_pairs={{0,8},{4,12},{8,0},{12,4},{1,9},{5,13},{9,1},{13,5},{2,10},{6,14},... | collective-permute-start | bytes 61448 | tf_op jit(solution)/shard_map/ppermute | solution.py:211
  124.0 14.9 %collective-permute-start.11 = (f32[5,1024]{1,0:T(8,128)S(1)}, f32[5,1024]{1,0:T(8,128)S(1)}, u32[]{:S(2)}, u32[]{:S(2)}) collective-permute-start(f32[5,1024]{1,0:T(8,128)S(1)} %stack.4), channel_id=1, source_target_pairs={{0,12},{4,0},{8,4},{12,8},{1,13},{5,1},{9,5},{13,9},{2,14},{6,2},{... | collective-permute-start | bytes 61448 | tf_op jit(solution)/shard_map/ppermute | solution.py:211
  125.5 13.4 %collective-permute-start.10 = (f32[5,1024]{1,0:T(8,128)S(1)}, f32[5,1024]{1,0:T(8,128)S(1)}, u32[]{:S(2)}, u32[]{:S(2)}) collective-permute-start(f32[5,1024]{1,0:T(8,128)S(1)} %stack.4), channel_id=1, source_target_pairs={{0,4},{4,8},{8,12},{12,0},{1,5},{5,9},{9,13},{13,1},{2,6},{6,10},{... | collective-permute-start | bytes 61448 | tf_op jit(solution)/shard_map/ppermute | solution.py:211
  153.3 8.3 %collective-permute-start.16 = (bf16[96,768]{1,0:T(8,128)(2,1)S(1)}, bf16[96,768]{1,0:T(8,128)(2,1)S(1)}, u32[]{:S(2)}, u32[]{:S(2)}) collective-permute-start(bf16[96,768]{1,0:T(8,128)(2,1)S(1)} %get-tuple-element.35), channel_id=1, source_target_pairs={{0,8},{4,12},{8,0},{12,4},{1,9},{5,13},{9,1},{13,5},{2,10},{6,14},... | collective-permute-start | bytes 442376 | tf_op jit(solution)/shard_map/ppermute | solution.py:243
  156.1 8.3 %collective-permute-start.15 = (bf16[96,768]{1,0:T(8,128)(2,1)S(1)}, bf16[96,768]{1,0:T(8,128)(2,1)S(1)}, u32[]{:S(2)}, u32[]{:S(2)}) collective-permute-start(bf16[96,768]{1,0:T(8,128)(2,1)S(1)} %get-tuple-element.36), channel_id=1, source_target_pairs={{0,12},{4,0},{8,4},{12,8},{1,13},{5,1},{9,5},{13,9},{2,14},{6,2},{... | collective-permute-start | bytes 442376 | tf_op jit(solution)/shard_map/ppermute | solution.py:243
  156.1 8.3 %collective-permute-start.14 = (bf16[96,768]{1,0:T(8,128)(2,1)S(1)}, bf16[96,768]{1,0:T(8,128)(2,1)S(1)}, u32[]{:S(2)}, u32[]{:S(2)}) collective-permute-start(bf16[96,768]{1,0:T(8,128)(2,1)S(1)} %get-tuple-element.34), channel_id=1, source_target_pairs={{0,4},{4,8},{8,12},{12,0},{1,5},{5,9},{9,13},{13,1},{2,6},{6,10},{... | collective-permute-start | bytes 442376 | tf_op jit(solution)/shard_map/ppermute | solution.py:243
  159.4 9.0 %collective-permute-start.20 = (f32[8,128]{0,1:T(8,128)S(1)}, f32[8,128]{0,1:T(8,128)S(1)}, u32[]{:S(2)}, u32[]{:S(2)}) collective-permute-start(f32[8,128]{0,1:T(8,128)S(1)} %broadcast_in_dim.58), channel_id=1, source_target_pairs={{0,1},{1,0},{2,3},{3,2},{4,5},{5,4},{6,7},{7,6},{8,9},{9,8},{10,11... | collective-permute-start | bytes 12296 | tf_op jit(solution)/shard_map/ppermute | solution.py:240
  164.4 8.1 %collective-permute-start.18 = (bf16[48,768]{1,0:T(8,128)(2,1)S(1)}, bf16[48,768]{1,0:T(8,128)(2,1)S(1)}, u32[]{:S(2)}, u32[]{:S(2)}) collective-permute-start(bf16[48,768]{1,0:T(8,128)(2,1)S(1)} %get-tuple-element.39), channel_id=1, source_target_pairs={{0,18},{2,0},{16,2},{18,16},{1,19},{3,1},{17,3},{19,17},{4,22},{6,... | collective-permute-start | bytes 221192 | tf_op jit(solution)/shard_map/ppermute | solution.py:249
  166.7 6.7 %collective-permute-start.17 = (bf16[48,768]{1,0:T(8,128)(2,1)S(1)}, bf16[48,768]{1,0:T(8,128)(2,1)S(1)}, u32[]{:S(2)}, u32[]{:S(2)}) collective-permute-start(bf16[48,768]{1,0:T(8,128)(2,1)S(1)} %get-tuple-element.39), channel_id=1, source_target_pairs={{0,2},{2,16},{16,18},{18,0},{1,3},{3,17},{17,19},{19,1},{4,6},{6,2... | collective-permute-start | bytes 221192 | tf_op jit(solution)/shard_map/ppermute | solution.py:249
  166.7 5.9 %collective-permute-start.19 = (bf16[48,768]{1,0:T(8,128)(2,1)S(1)}, bf16[48,768]{1,0:T(8,128)(2,1)S(1)}, u32[]{:S(2)}, u32[]{:S(2)}) collective-permute-start(bf16[48,768]{1,0:T(8,128)(2,1)S(1)} %get-tuple-element.40), channel_id=1, source_target_pairs={{0,16},{2,18},{16,0},{18,2},{1,17},{3,19},{17,1},{19,3},{4,20},{6,... | collective-permute-start | bytes 221192 | tf_op jit(solution)/shard_map/ppermute | solution.py:249
  173.5 5.9 %collective-permute-start.21 = (f32[56,768]{1,0:T(8,128)S(1)}, f32[56,768]{1,0:T(8,128)S(1)}, u32[]{:S(2)}, u32[]{:S(2)}) collective-permute-start(f32[56,768]{1,0:T(8,128)S(1)} %pad_maximum_fusion.3), channel_id=1, source_target_pairs={{0,32},{32,0},{64,96},{96,64},{128,160},{160,128},{192,224},{224,1... | collective-permute-start | bytes 516104 | tf_op jit(solution)/shard_map/ppermute | solution.py:253
  179.5 9.6 %collective-permute-start.22 = (f32[56,768]{1,0:T(8,128)S(1)}, f32[56,768]{1,0:T(8,128)S(1)}, u32[]{:S(2)}, u32[]{:S(2)}) collective-permute-start(f32[56,768]{1,0:T(8,128)S(1)} %fusion.19), channel_id=1, source_target_pairs={{0,64},{32,96},{64,0},{96,32},{128,192},{160,224},{192,128},{224,1... | collective-permute-start | bytes 516104 | tf_op jit(solution)/shard_map/ppermute | solution.py:253
  189.1 12.4 %collective-permute-start.23 = (f32[56,768]{1,0:T(8,128)S(1)}, f32[56,768]{1,0:T(8,128)S(1)}, u32[]{:S(2)}, u32[]{:S(2)}) collective-permute-start(f32[56,768]{1,0:T(8,128)S(1)} %add.384), channel_id=1, source_target_pairs={{0,128},{32,160},{64,192},{96,224},{128,0},{160,32},{192,64},{224,... | collective-permute-start | bytes 516104 | tf_op jit(solution)/shard_map/ppermute | solution.py:253
  (11 other events, 74.5 us)
Sparse Core Ops, SparseCore 0:
  11.8 42.1 all-gather.4
  55.8 38.2 all-gather.2

commit v2 on v0

v2 whole, which is shorter than its diff:
```python
import functools

import jax
import jax.numpy as jnp
import numpy as np
from jax import lax
from jax.experimental import pallas as pl
from jax.experimental.pallas import tpu as pltpu
from jax.sharding import Mesh, PartitionSpec as P

sig_scale = 10.0
sig_bias = -10.0
teacher_gain = 3.0
eps_value = 1e-06

F32 = jnp.float32
BF16 = jnp.bfloat16
LOG2E = float(np.log2(np.e))
LN2 = float(np.log(2.0))
NT = (((1,), (1,)), ((), ()))
ALL = ("z", "yh", "x", "yl", "c")
Y = ("yh", "yl")
VMEM_LIMIT = 48 * 1024 * 1024
LANES = 128
STEP = 32


def ring(n, k):
    return [(i, (i + k) % n) for i in range(n)]


def flip(n, k):
    return [(i, i ^ k) for i in range(n)]


SMEM = pl.BlockSpec(memory_space=pltpu.SMEM)
VMEM = pl.BlockSpec(memory_space=pltpu.VMEM)


def shape(dims, dtype):
    return jax.ShapeDtypeStruct(dims, dtype)


def params():
    return pltpu.CompilerParams(vmem_limit_bytes=VMEM_LIMIT)


def cost(macs, megabytes, exps=0):
    return pl.CostEstimate(flops=int(2 * macs), bytes_accessed=int(megabytes * 1e6), transcendentals=int(exps))


def images_kernel(zn, dt, place_ref, own_txt_ref, proj_ref, *refs):
    pieces, (timg_ref, feat_ref, simg_ref, simgb_ref, inv_ref, self_ref, diag_ref) = refs[:zn], refs[zn:]
    rows = pieces[0].shape[0]
    z = place_ref[0]
    for k, piece in enumerate(pieces):
        at = pl.ds(pl.multiple_of(lax.rem(z + zn - k, zn) * rows, rows), rows)
        timg_ref[at, :] = piece[:, :dt]
        feat_ref[at, :] = piece[:, dt:]
    pre = jnp.dot(feat_ref[...], proj_ref[...], preferred_element_type=F32)
    norm = jnp.sqrt(jnp.sum(pre * pre, axis=1, keepdims=True) + eps_value)
    simg = pre / norm
    simg_ref[...] = simg
    simgb_ref[...] = simg.astype(BF16)
    inv_ref[...] = jnp.broadcast_to(1.0 / norm, inv_ref.shape)
    own = pl.ds(pl.multiple_of(z * rows, rows), rows)
    s = simg_ref[own, :]
    txt = own_txt_ref[...].astype(F32)
    margin = sig_scale * jnp.sum(s.astype(BF16).astype(F32) * txt, axis=1, keepdims=True) + sig_bias
    self_ref[...] = jnp.zeros_like(self_ref)
    self_ref[own, :] = jnp.broadcast_to(-margin, (rows, LANES))
    d = -sig_scale * txt
    diag_ref[...] = (d - s * jnp.sum(s * d, axis=1, keepdims=True)) * inv_ref[own, 0:1]


def make_block(first, gain, sizes):
    def kernel(timg_ref, simgb_ref, old_ref, *refs):
        texts, refs = refs[:len(sizes)], refs[len(sizes):]
        if not first:
            refs = refs[4:]
        te_ref, se_ref, sig_ref, stu_ref, stat_ref, flat_ref, tl, sl = refs
        dt = timg_ref.shape[1]
        at = 0
        for ref, n in zip(texts, sizes):
            tl[:, at:at + n] = lax.dot_general(timg_ref[...], ref[:, :dt], NT, preferred_element_type=F32)
            sl[:, at:at + n] = lax.dot_general(simgb_ref[...], ref[:, dt:], NT, preferred_element_type=F32)
            stu_ref[at:at + n, :] = ref[:, dt:]
            at += n
        lane = lax.broadcasted_iota(jnp.int32, (STEP, LANES), 1)
        shrink = float(np.exp(sig_bias))
        for r in range(0, timg_ref.shape[0], STEP):
            rows = slice(r, r + STEP)
            t = (gain * LOG2E) * tl[rows, :]
            s = (sig_scale * LOG2E) * sl[rows, :]
            old = old_ref[rows, :]
            top = jnp.max(t, axis=1, keepdims=True)
            if not first:
                top = jnp.maximum(top, old[:, 0:1])
            te = jnp.exp2(t - top)
            se = jnp.exp2(s)
            em = se * shrink
            up = 1.0 + em
            sig = em * pl.reciprocal(up, approx=True)
            soft = jnp.log(up) + (em - (up - 1.0))
            te_ref[rows, :] = te.astype(BF16)
            se_ref[rows, :] = se.astype(BF16)
            sig_ref[rows, :] = sig.astype(BF16)
            total = lambda v: jnp.sum(v, axis=1, keepdims=True)
            sums = [total(te), total(se), total(te * (t - s)), total(soft)]
            if first:
                sums[3] = sums[3] + old[:, 0:1]
            else:
                w = jnp.exp2(old[:, 0:1] - top)
                sums = [sums[0] + w * old[:, 1:2], sums[1] + old[:, 2:3], sums[2] + w * old[:, 3:4], sums[3] + old[:, 4:5]]
            stat = jnp.broadcast_to(top, (STEP, LANES))
            for n, v in enumerate(sums):
                stat = jnp.where(lane == n + 1, v, stat)
            stat_ref[rows, :] = stat
        flat_ref[...] = stat_ref[...].T[:8, :]

    return kernel


def embed_kernel(blocks, te_ref, se_ref, sig_ref, stu_ref, simg_ref, inv_ref, feat_ref, *refs):
    stats, (a_ref, b_ref, c_ref, ft_ref, scaled) = refs[:blocks], refs[blocks:]
    span = te_ref.shape[1] // blocks
    top = stats[-1][:, 0:1]
    for n in range(blocks):
        cols = slice(n * span, (n + 1) * span)
        w = jnp.exp2(stats[n][:, 0:1] - top)
        scaled[:, cols] = (te_ref[:, cols].astype(F32) * w).astype(BF16)
    simg = simg_ref[...]
    inv = inv_ref[:, 0:1]
    for src, dst in ((sig_ref, c_ref), (se_ref, a_ref), (scaled, b_ref)):
        d = jnp.dot(src[...], stu_ref[...], preferred_element_type=F32)
        along = jnp.sum(simg * d, axis=1, keepdims=True)
        dst[...] = ((d - simg * along) * inv).astype(BF16)
    ft_ref[...] = feat_ref[...].T


def away_kernel(place_ref, sums_ref, flat_ref, a_ref, b_ref, c_ref, diag_ref, ft_ref,
                out_ref, hi_ref, lo_ref, val_ref, turned, grad, cut_ft):
    rows = diag_ref.shape[0]
    half, ds = grad.shape[0], a_ref.shape[1]
    top, tsum, ssum, tval, soft = (sums_ref[k:k + 1, :] for k in range(5))
    value = tval / tsum * LN2 + soft - (top * LN2 + jnp.log(tsum)) + jnp.log(ssum)
    val_ref[...] = jnp.broadcast_to(value, val_ref.shape)
    ca = sig_scale / ssum
    cb = -sig_scale * jnp.exp2(flat_ref[0:1, :] - top) / tsum
    row = lax.broadcasted_iota(jnp.int32, (LANES, ca.shape[1]), 0)
    turned[...] = jnp.where(row == 0, ca, cb).T
    d = turned[:, 0:1] * a_ref[...].astype(F32) + turned[:, 1:2] * b_ref[...].astype(F32) + sig_scale * c_ref[...].astype(F32)
    images = d.shape[0]
    grad_d = d
    hi_ref[...] = grad_d.astype(BF16)
    lo_ref[...] = (grad_d - hi_ref[...].astype(F32)).astype(BF16)
    own = pl.ds(pl.multiple_of(place_ref[0] * rows, rows), rows)
    mine = hi_ref[own, :].astype(F32) + lo_ref[own, :].astype(F32) + diag_ref[...]
    mine_hi = mine.astype(BF16)
    hi_ref[own, :] = mine_hi
    lo_ref[own, :] = (mine - mine_hi.astype(F32)).astype(BF16)
    pick(cut_ft, ft_ref, 1 - place_ref[1])
    g = jnp.dot(cut_ft[...], hi_ref[...], preferred_element_type=F32)
    g = g + jnp.dot(cut_ft[...], lo_ref[...], preferred_element_type=F32)
    out_ref[:half, :] = g
    out_ref[half:, :] = jnp.broadcast_to(jnp.sum(value, axis=1, keepdims=True), (8, ds))


def pick(dst, src, core):
    groups = 8
    cut = dst.shape[0] // groups
    for g in range(groups):
        dst[g * cut:(g + 1) * cut, :] = src[pl.ds(pl.multiple_of((2 * g + core) * cut, cut), cut), :]


def home_kernel(place_ref, ft_ref, hi_ref, lo_ref, out_ref, cut_ft):
    pick(cut_ft, ft_ref, place_ref[1])
    out_ref[...] = jnp.dot(cut_ft[...], hi_ref[...], preferred_element_type=F32) + jnp.dot(
        cut_ft[...], lo_ref[...], preferred_element_type=F32)


def cores_kernel(xn, place_ref, home_ref, got_ref, away_ref, keep_ref, *sends):
    half = home_ref.shape[0]
    cut = half // xn
    loss = got_ref[half:, :] + away_ref[...]
    x = place_ref[2]
    at = pl.ds(pl.multiple_of(x * cut, cut), cut)
    keep_ref[:cut, :] = home_ref[at, :] + got_ref[at, :]
    keep_ref[cut:, :] = loss
    hi = loss.astype(BF16).astype(F32)
    mid = (loss - hi).astype(BF16).astype(F32)
    low = loss - hi - mid
    row = lax.broadcasted_iota(jnp.int32, loss.shape, 0)
    packed = jnp.where(row == 0, hi, jnp.where(row == 1, mid, jnp.where(row == 2, low, 0.0)))
    packed = jnp.concatenate([packed, jnp.zeros_like(packed)], axis=0).astype(BF16)
    for k, ref in zip((1, 3, 2), sends):
        at = pl.ds(pl.multiple_of(lax.rem(x + k, xn) * cut, cut), cut)
        ref[:cut, :] = (home_ref[at, :] + got_ref[at, :]).astype(BF16)
        ref[cut:, :] = packed


def rows_kernel(place_ref, keep_ref, p_ref, q_ref, r_ref, mine_ref, other_ref, total):
    cut = keep_ref.shape[0] - 8
    half = cut // 2
    total[...] = keep_ref[:cut, :]
    loss = keep_ref[cut:, :]
    for ref in (p_ref, q_ref, r_ref):
        total[...] += ref[:cut, :].astype(F32)
        packed = ref[cut:, :].astype(F32)
        loss = loss + (packed[0:1, :] + packed[1:2, :] + packed[2:3, :])
    y = place_ref[3]
    for ref, at in ((mine_ref, y), (other_ref, 1 - y)):
        ref[:half, :] = total[pl.ds(pl.multiple_of(at * half, half), half), :]
        ref[half:, :] = loss


def merge(*parts):
    top = functools.reduce(jnp.maximum, [p[0] for p in parts])
    out = [0.0] * 4
    for p in parts:
        w = jnp.exp2(p[0] - top)
        out = [out[0] + w * p[1], out[1] + p[2], out[2] + w * p[3], out[3] + p[4]]
    return jnp.stack([top] + out)


def per_device(features, proj, student_text, teacher_image, teacher_text):
    rows, feat = features.shape
    dt = teacher_text.shape[1]
    ds = student_text.shape[1]
    zn, yn, xn, cn = (lax.axis_size(a) for a in ("z", Y, "x", "c"))
    images = rows * zn
    batch = images * yn * xn * cn
    texts = rows * yn * xn * cn
    column = rows * yn
    gain = float(teacher_gain / np.sqrt(np.float32(dt)))
    half = feat // cn
    place = jnp.stack([lax.axis_index(a) for a in ("z", "c", "x", "yl")]).astype(jnp.int32)

    img = jnp.concatenate([teacher_image, features], axis=1)
    st = student_text.astype(F32)
    st_own = (st / jnp.sqrt(jnp.sum(st * st, axis=-1, keepdims=True) + eps_value)).astype(BF16)
    txt = jnp.concatenate([teacher_text, st_own], axis=1)

    up, down = [img], [img]
    for _ in range(zn // 2):
        up.append(lax.ppermute(up[-1], "z", ring(zn, 1)))
    for _ in range(zn // 2 - 1):
        down.append(lax.ppermute(down[-1], "z", ring(zn, zn - 1)))
    pieces = up + down[:0:-1]

    swap = lambda v: lax.ppermute(v, "c", flip(cn, 1))
    left = lax.ppermute(txt, Y, ring(yn, 1))
    right = lax.ppermute(txt, Y, ring(yn, yn - 1))
    far = lax.ppermute(left, Y, ring(yn, 1))
    own_col = jnp.concatenate([txt, left, right, far], axis=0)
    left_col = lax.ppermute(own_col, "x", ring(xn, 1))
    right_col = lax.ppermute(own_col, "x", ring(xn, xn - 1))
    far_a = lax.ppermute(left_col[:column // 2], "x", ring(xn, 1))
    far_b = lax.ppermute(right_col[column // 2:], "x", ring(xn, xn - 1))
    blocks = [(own_col,), (left_col,), (right_col,), (far_a, far_b)]
    blocks = [b + tuple(swap(v) for v in b) for b in blocks]

    timg, feats, simg, simgb, inv, self_col, diag = pl.pallas_call(
        functools.partial(images_kernel, zn, dt),
        in_specs=[SMEM] + [VMEM] * (2 + zn),
        out_specs=[VMEM] * 7,
        out_shape=[shape((images, dt), BF16), shape((images, feat), BF16), shape((images, ds), F32), shape((images, ds), BF16),
                   shape((images, LANES), F32), shape((images, LANES), F32), shape((rows, ds), F32)],
        compiler_params=params(),
        cost_estimate=cost(images * feat * ds, 9),
        name="images",
    )(place, st_own, proj, *pieces)

    span = column * cn
    part = images // 2
    by_rows = lambda n: pl.BlockSpec((part, n), lambda i: (i, 0))
    old = self_col
    chain = []
    cols = []
    for n, block in enumerate(blocks):
        first = n == 0
        at = lambda i, n=n: (i, n)
        big = [shape((images, texts), BF16)] * 3 + [shape((texts, ds), BF16)]
        out = pl.pallas_call(
            make_block(first, gain, [v.shape[0] for v in block]),
            grid=(2,),
            in_specs=[by_rows(dt), by_rows(ds), by_rows(LANES)]
            + [pl.BlockSpec(v.shape, lambda i: (0, 0)) for v in block]
            + ([] if first else [pl.BlockSpec(memory_space=pl.ANY)] * 4),
            out_specs=[pl.BlockSpec((part, span), at)] * 3 + [pl.BlockSpec((span, ds), lambda i, n=n: (n, 0)), by_rows(LANES), pl.BlockSpec((8, part), lambda i: (0, i))],
            out_shape=big + [shape((images, LANES), F32), shape((8, images), F32)],
            scratch_shapes=[pltpu.VMEM((part, span), F32)] * 2,
            input_output_aliases={} if first else {3 + len(block) + k: k for k in range(4)},
            compiler_params=params(),
            cost_estimate=cost(images * span * (dt + ds), 7, 4 * images * span),
            name="block" + str(n),
        )(timg, simgb, old, *block, *chain)
        chain, old, flat = list(out[:4]), out[4], out[5]
        cols.append(old)

    a, b, c, ft = pl.pallas_call(
        functools.partial(embed_kernel, len(cols)),
        grid=(2,),
        in_specs=[by_rows(texts)] * 3 + [pl.BlockSpec((texts, ds), lambda i: (0, 0)), by_rows(ds), by_rows(LANES), by_rows(feat)] + [by_rows(LANES)] * len(cols),
        out_specs=[by_rows(ds)] * 3 + [pl.BlockSpec((feat, part), lambda i: (0, i))],
        out_shape=[shape((images, ds), BF16)] * 3 + [shape((feat, images), BF16)],
        scratch_shapes=[pltpu.VMEM((part, texts), BF16)],
        compiler_params=params(),
        cost_estimate=cost(3 * images * texts * ds, 16),
        name="embed",
    )(*chain, simg, inv, feats, *cols)

    own = flat[:5]
    below = lax.ppermute(own, "z", ring(zn, 1))
    above = lax.ppermute(own, "z", ring(zn, zn - 1))
    pair = merge(own, above)
    window = merge(pair, below)
    ahead = lax.ppermute(window, "z", ring(zn, zn - 3))
    behind = lax.ppermute(pair, "z", ring(zn, 3))
    sums = merge(window, ahead, behind)

    away, hi, lo, val = pl.pallas_call(
        away_kernel,
        in_specs=[SMEM] + [VMEM] * 7,
        out_specs=[VMEM] * 4,
        out_shape=[shape((half + 8, ds), F32), shape((images, ds), BF16), shape((images, ds), BF16), shape((8, images), F32)],
        scratch_shapes=[pltpu.VMEM((images, LANES), F32), pltpu.VMEM((half, ds), F32), pltpu.VMEM((half, images), BF16)],
        compiler_params=params(),
        cost_estimate=cost(2 * images * half * ds, 8),
        name="away",
    )(place, sums, flat, a, b, c, diag, ft)
    arrived = swap(away)
    home = pl.pallas_call(
        home_kernel,
        in_specs=[SMEM] + [VMEM] * 3,
        out_specs=VMEM,
        out_shape=shape((half, ds), F32),
        scratch_shapes=[pltpu.VMEM((half, images), BF16)],
        compiler_params=params(),
        cost_estimate=cost(2 * images * half * ds, 4),
        name="home",
    )(place, ft, hi, lo)

    cut = half // xn
    keep, *sends = pl.pallas_call(
        functools.partial(cores_kernel, xn),
        in_specs=[SMEM] + [VMEM] * 3,
        out_specs=[VMEM] * 4,
        out_shape=[shape((cut + 8, ds), F32)] + [shape((cut + 16, ds), BF16)] * 3,
        compiler_params=params(),
        name="cores",
    )(place, home, arrived, away[half:])
    got = [lax.ppermute(v, "x", ring(xn, k)) for k, v in zip((1, 3, 2), sends)]
    mine, other = pl.pallas_call(
        rows_kernel,
        in_specs=[SMEM] + [VMEM] * 4,
        out_specs=[VMEM] * 2,
        out_shape=[shape((cut // 2 + 8, ds), F32)] * 2,
        scratch_shapes=[pltpu.VMEM((cut, ds), F32)],
        compiler_params=params(),
        name="rows",
    )(place, keep, *got)
    got = [lax.ppermute(other, Y, ring(yn, k)) for k in (1, 3)] + [lax.ppermute(mine, Y, ring(yn, 2))]
    plane = mine + got[0] + got[1] + got[2]

    below = lax.ppermute(plane, "z", ring(zn, 1))
    above = lax.ppermute(plane, "z", ring(zn, zn - 1))
    pair = plane + above
    window = pair + below
    ahead = lax.ppermute(window, "z", ring(zn, zn - 3))
    behind = lax.ppermute(pair, "z", ring(zn, 3))
    total = window + ahead + behind

    row_loss = lax.dynamic_slice_in_dim(val[0], lax.axis_index("z") * rows, rows, 0)
    return (row_loss, total[cut // 2, 0] / (batch * zn), total[:cut // 2])


def solution(mesh):
    sizes = dict(mesh.shape)
    fine = Mesh(np.asarray(mesh.devices).reshape(sizes["blk"] // 2, 2, sizes["img"] // 4, 2, 2), ALL)
    return jax.shard_map(
        per_device,
        mesh=fine,
        in_specs=(P(ALL, None), P(), P(ALL, None), P(ALL, None), P(ALL, None)),
        out_specs=(P(ALL), P(), P(("x", "yl", "c"), None)),
        check_vma=False,
    )
```

time: 564 us -> 184 us (0.33)
  waiting for transfers between devices: 342 us -> 72.4 us
  blocking collectives: 157 us -> 0 us
  starting transfers between devices: 0.24 us -> 44 us
  Pallas kernels: 0 us -> 39.5 us
  matrix products: 30.9 us -> 0 us
  between operations: 16.7 us -> 2.8 us
  local copies, waits for them, and re-layouts: 6.21 us -> 18.6 us
  other arithmetic: 10.4 us -> 4.25 us
    all_gather x3 -> x0, waiting for transfers between devices: 135 us -> none  [the longest x1 99.8 us: per_device(): text_all = lax.all_gather(text_pair, 'blk', axis=0, tiled=True)]
    psum x2 -> x0, blocking collectives: 107 us -> none  [the longest x1 81.2 us: per_device(): lax.psum(jnp.sum(row_loss), ('blk', 'img')) / (rows * span * cycle_size)]
    psum x1 -> x0, waiting for transfers between devices: 79 us -> none  [per_device(): grad_proj = lax.psum(grad_rows, 'blk')]
    ppermute x0 -> x34, waiting for transfers between devices: none -> 72.4 us  [the longest x4 13.1 us: per_device(): up.append(lax.ppermute(up[-1], 'z', ring(zn, 1)))]
    unnamed x7 -> x0, waiting for transfers between devices: 65.8 us -> none
    reduce_scatter x1 -> x0, waiting for transfers between devices: 62.7 us -> none  [per_device(): d_own = lax.psum_scatter(d_simg, 'img', scatter_dimension=0, tiled=True)]
    ppermute x0 -> x34, starting transfers between devices: none -> 44 us  [the longest x3 10.6 us: per_device(): down.append(lax.ppermute(down[-1], 'z', ring(zn, zn - 1)))]
    pallas_call x0 -> x10, Pallas kernels: none -> 39.5 us  [the longest x4 21.7 us: per_device(): pl.pallas_call(make_block(first, gain, [v.shape[0] for v in block]), grid...]
  transfers between devices with their start and end apart: 6 -> 34, of which waited for: 5 -> 20; matrix products, arithmetic and copies ran while one was open for 3% -> 0% of each run, Pallas kernels for 0% -> 17%
where the time goes in v2:
time: 184 us; the launch traced here: 182 us
  waiting for transfers between devices  72.4 us (39%)
  starting transfers between devices  44 us (24%)
  Pallas kernels  39.5 us (21%)
  local copies, waits for them, and re-layouts  18.6 us (10%)
  other arithmetic  4.25 us (2%)
  between operations  2.8 us (2%)
    pallas_call x4, Pallas kernels, per_device(): pl.pallas_call(make_block(first, gain, [v.shape[0] for v in block]), grid...  21.7 us
    unnamed x65, local copies, waits for them, and re-layouts  16.7 us
    ppermute x4, waiting for transfers between devices, per_device(): up.append(lax.ppermute(up[-1], 'z', ring(zn, 1)))  13.1 us
    ppermute x3, starting transfers between devices, per_device(): down.append(lax.ppermute(down[-1], 'z', ring(zn, zn - 1)))  10.6 us
    pallas_call x1, Pallas kernels, per_device(): pl.pallas_call(functools.partial(embed_kernel, len(cols)), grid=(2,), in_...  9.5 us
    ppermute x3, waiting for transfers between devices, per_device(): got = [lax.ppermute(v, 'x', ring(xn, k)) for k, v in zip((1, 3, 2), sends)]  7.8 us
    ppermute x1, waiting for transfers between devices, per_device(): far = lax.ppermute(left, Y, ring(yn, 1))  7.45 us
    ppermute x2, waiting for transfers between devices, per_device(): lax.ppermute(other, Y, ring(yn, k))  7.07 us
  transfers between devices with their start and end apart: 34, of which 20 were waited for; matrix products, arithmetic and copies ran while one was open for 0% of the time, Pallas kernels for 17%

profile of v2, /device:TPU:2, one launch (start us, length us, event | category | flops | bytes accessed | tf_op | source)
XLA Modules:
  0.0 181.6 jit_solution(9234135810407060571)
XLA Ops:
  7.0 5.4 %collective-permute-done.7 = bf16[64,1792]{1,0:T(8,128)(2,1)S(1)} collective-permute-done((bf16[64,1792]{1,0:T(8,128)(2,1)S(1)}, bf16[64,1792]{1,0:T(8,128)(2,1)S(1)}, u32[]{:S(2)}, u32[]{:S(2)}) %collective-permute-start.7) | collective-permute-done | bytes 229408 | tf_op jit(solution)/shard_map/ppermute | solution.py:252
  12.6 7.4 %collective-permute-done.9 = bf16[64,1792]{1,0:T(8,128)(2,1)S(1)} collective-permute-done((bf16[64,1792]{1,0:T(8,128)(2,1)S(1)}, bf16[64,1792]{1,0:T(8,128)(2,1)S(1)}, u32[]{:S(2)}, u32[]{:S(2)}) %collective-permute-start.9) | collective-permute-done | bytes 229408 | tf_op jit(solution)/shard_map/ppermute | solution.py:254
  25.3 4.0 %collective-permute-start.4 = (bf16[64,1792]{1,0:T(8,128)(2,1)S(1)}, bf16[64,1792]{1,0:T(8,128)(2,1)S(1)}, u32[]{:S(2)}, u32[]{:S(2)}) collective-permute-start(bf16[64,1792]{1,0:T(8,128)(2,1)S(1)} %constant_dynamic-update-slice_fusion.refs_0_), channel_id=1, source_target_pairs={{0,224},{32,0},{64,32},{96,64},{128,96},{160,128},{192,160},{224,1... | collective-permute-start | bytes 688136 | tf_op jit(solution)/shard_map/ppermute | solution.py:248
  29.3 3.9 %collective-permute-done.refs_1_ = bf16[64,1792]{1,0:T(8,128)(2,1)S(1)} collective-permute-done((bf16[64,1792]{1,0:T(8,128)(2,1)S(1)}, bf16[64,1792]{1,0:T(8,128)(2,1)S(1)}, u32[]{:S(2)}, u32[]{:S(2)}) %collective-permute-start) | collective-permute-done | bytes 229408 | tf_op jit(solution)/shard_map/ppermute | solution.py:246
  33.9 3.2 %collective-permute-start.5 = (bf16[64,1792]{1,0:T(8,128)(2,1)S(1)}, bf16[64,1792]{1,0:T(8,128)(2,1)S(1)}, u32[]{:S(2)}, u32[]{:S(2)}) collective-permute-start(bf16[64,1792]{1,0:T(8,128)(2,1)S(1)} %collective-permute-done.4.refs_7_), channel_id=1, source_target_pairs={{0,224},{32,0},{64,32},{96,64},{128,96},{160,128},{192,160},{224,1... | collective-permute-start | bytes 688136 | tf_op jit(solution)/shard_map/ppermute | solution.py:248
  37.8 3.2 %collective-permute-done.1.refs_2_ = bf16[64,1792]{1,0:T(8,128)(2,1)S(1)} collective-permute-done((bf16[64,1792]{1,0:T(8,128)(2,1)S(1)}, bf16[64,1792]{1,0:T(8,128)(2,1)S(1)}, u32[]{:S(2)}, u32[]{:S(2)}) %collective-permute-start.1) | collective-permute-done | bytes 229408 | tf_op jit(solution)/shard_map/ppermute | solution.py:246
  41.7 3.3 %collective-permute-start.6 = (bf16[64,1792]{1,0:T(8,128)(2,1)S(1)}, bf16[64,1792]{1,0:T(8,128)(2,1)S(1)}, u32[]{:S(2)}, u32[]{:S(2)}) collective-permute-start(bf16[64,1792]{1,0:T(8,128)(2,1)S(1)} %collective-permute-done.5.refs_6_), channel_id=1, source_target_pairs={{0,224},{32,0},{64,32},{96,64},{128,96},{160,128},{192,160},{224,1... | collective-permute-start | bytes 688136 | tf_op jit(solution)/shard_map/ppermute | solution.py:248
  45.1 3.2 %collective-permute-done.2.refs_3_ = bf16[64,1792]{1,0:T(8,128)(2,1)S(1)} collective-permute-done((bf16[64,1792]{1,0:T(8,128)(2,1)S(1)}, bf16[64,1792]{1,0:T(8,128)(2,1)S(1)}, u32[]{:S(2)}, u32[]{:S(2)}) %collective-permute-start.2) | collective-permute-done | bytes 229408 | tf_op jit(solution)/shard_map/ppermute | solution.py:246
  57.3 5.9 %collective-permute-done.15.refs_0_ = bf16[128,1792]{1,0:T(8,128)(2,1)S(1)} collective-permute-done((bf16[128,1792]{1,0:T(8,128)(2,1)S(1)}, bf16[128,1792]{1,0:T(8,128)(2,1)S(1)}, u32[]{:S(2)}, u32[]{:S(2)}) %collective-permute-start.15) | collective-permute-done | bytes 458784 | tf_op jit(solution)/shard_map/ppermute | solution.py:258
  71.9 3.6 %images.1 = (bf16[512,1024]{1,0:T(8,128)(2,1)S(1)}, bf16[512,768]{1,0:T(8,128)(2,1)S(1)}, f32[512,768]{1,0:T(8,128)}, bf16[512,768]{1,0:T(8,128)(2,1)S(1)}, f32[...) custom-call(s32[4]{0:T(128)S(1)} %pad_add_fusion.place_ref, ...), custom_call_target="tpu_custom_call" | custom-call | flops 603979776 | bytes 9000000 | tf_op jit(solution)/shard_map/images/pallas_call | solution.py:263
  75.6 5.5 %block0.1 = (bf16[512,2048]{1,0:T(8,128)(2,1)}, bf16[512,2048]{1,0:T(8,128)(2,1)}, bf16[512,2048]{1,0:T(8,128)(2,1)}, bf16[2048,768]{1,0:T(8,128)(2,1)}, f32[512,128]{1,0:T(8,128)S(1)}, /*index=5*/f32[8,512]{1,0:T(8,128)}) custom-call(bf16[512,1024]{1,0:T(8,128)(2,1)S(1)} %get-tuple-element.45.timg_ref, bf16[512,768]{1,0:T(8,128)(2,1)S(1)} %get-tuple-element.46.simgb_ref, ...), custom_call_target="tpu_custom_call" | custom-call | flops 939524096 | bytes 7000000 | tf_op jit(solution)/shard_map/block0/pallas_call | solution.py:284
  81.1 5.1 %block1.1 = (bf16[512,2048]{1,0:T(8,128)(2,1)}, bf16[512,2048]{1,0:T(8,128)(2,1)}, bf16[512,2048]{1,0:T(8,128)(2,1)}, bf16[2048,768]{1,0:T(8,128)(2,1)}, f32[512,128]{1,0:T(8,128)S(1)}, /*index=5*/f32[8,512]{1,0:T(8,128)}) custom-call(bf16[512,1024]{1,0:T(8,128)(2,1)S(1)} %get-tuple-element.4, ...), custom_call_target="tpu_custom_call", output_to_operand_aliasing={{0}: (5, {}), {1}: (6, {}), {2}: (7, {}), {3}: (8, {})} | custom-call | flops 939524096 | bytes 7000000 | tf_op jit(solution)/shard_map/block1/pallas_call | solution.py:284
  86.2 5.2 %block2.1 = (bf16[512,2048]{1,0:T(8,128)(2,1)}, bf16[512,2048]{1,0:T(8,128)(2,1)}, bf16[512,2048]{1,0:T(8,128)(2,1)}, bf16[2048,768]{1,0:T(8,128)(2,1)}, f32[512,128]{1,0:T(8,128)S(1)}, /*index=5*/f32[8,512]{1,0:T(8,128)}) custom-call(bf16[512,1024]{1,0:T(8,128)(2,1)S(1)} %get-tuple-element.4, ...), custom_call_target="tpu_custom_call", output_to_operand_aliasing={{0}: (5, {}), {1}: (6, {}), {2}: (7, {}), {3}: (8, {})} | custom-call | flops 939524096 | bytes 7000000 | tf_op jit(solution)/shard_map/block2/pallas_call | solution.py:284
  91.4 6.0 %block3.1 = (bf16[512,2048]{1,0:T(8,128)(2,1)}, bf16[512,2048]{1,0:T(8,128)(2,1)}, bf16[512,2048]{1,0:T(8,128)(2,1)}, bf16[2048,768]{1,0:T(8,128)(2,1)}, f32[512,128]{1,0:T(8,128)S(1)}, /*index=5*/f32[8,512]{1,0:T(8,128)S(1)}) custom-call(bf16[512,1024]{1,0:T(8,128)(2,1)S(1)} %get-tuple-element, ...), custom_call_target="tpu_custom_call", output_to_operand_aliasing={{0}: (7, {}), {1}: (8, {}), {2}: (9, {}), {3}: (10, {})} | custom-call | flops 939524096 | bytes 7000000 | tf_op jit(solution)/shard_map/block3/pallas_call | solution.py:284
  98.1 3.7 %collective-permute-start.19 = (f32[5,512]{1,0:T(8,128)S(1)}, f32[5,512]{1,0:T(8,128)S(1)}, u32[]{:S(2)}, u32[]{:S(2)}) collective-permute-start(f32[5,512]{1,0:T(8,128)S(1)} %bitcast.8), channel_id=1, source_target_pairs={{0,224},{32,0},{64,32},{96,64},{128,96},{160,128},{192,160},{224,1... | collective-permute-start | bytes 30728 | tf_op jit(solution)/shard_map/ppermute | solution.py:315
  103.3 3.5 %collective-permute-done.20 = f32[5,512]{1,0:T(8,128)S(1)} collective-permute-done((f32[5,512]{1,0:T(8,128)S(1)}, f32[5,512]{1,0:T(8,128)S(1)}, u32[]{:S(2)}, u32[]{:S(2)}) %collective-permute-start.20) | collective-permute-done | bytes 10272 | tf_op jit(solution)/shard_map/ppermute | solution.py:314
  117.0 9.5 %embed.1 = (bf16[512,768]{1,0:T(8,128)(2,1)S(1)}, bf16[512,768]{1,0:T(8,128)(2,1)S(1)}, bf16[512,768]{1,0:T(8,128)(2,1)S(1)}, bf16[768,512]{1,0:T(8,128)(2,1)S(1)}) custom-call(bf16[512,2048]{1,0:T(8,128)(2,1)} %get-tuple-element.64.te_ref, bf16[512,2048]{1,0:T(8,128)(2,1)} %get-tuple-element.65.se_ref, bf16[512,2048]{1,0:T(8,128)(2,1)} %get-tuple-element.66.sig_ref, ...), custom_call_target="tpu_custom_call" | custom-call | flops 4831838208 | bytes 16000000 | tf_op jit(solution)/shard_map/embed/pallas_call | solution.py:301
  134.5 2.9 %collective-permute-start.26 = (bf16[112,768]{1,0:T(8,128)(2,1)S(1)}, bf16[112,768]{1,0:T(8,128)(2,1)S(1)}, u32[]{:S(2)}, u32[]{:S(2)}) collective-permute-start(bf16[112,768]{1,0:T(8,128)(2,1)S(1)} %get-tuple-element.84), channel_id=1, source_target_pairs={{0,8},{4,12},{8,0},{12,4},{1,9},{5,13},{9,1},{13,5},{2,10},{6,14},... | collective-permute-start | bytes 516104 | tf_op jit(solution)/shard_map/ppermute | solution.py:353
  140.4 4.9 %collective-permute-done.26.r_ref = bf16[112,768]{1,0:T(8,128)(2,1)S(1)} collective-permute-done((bf16[112,768]{1,0:T(8,128)(2,1)S(1)}, bf16[112,768]{1,0:T(8,128)(2,1)S(1)}, u32[]{:S(2)}, u32[]{:S(2)}) %collective-permute-start.26) | collective-permute-done | bytes 172064 | tf_op jit(solution)/shard_map/ppermute | solution.py:353
  146.0 3.2 %collective-permute-start.28 = (f32[56,768]{1,0:T(8,128)S(1)}, f32[56,768]{1,0:T(8,128)S(1)}, u32[]{:S(2)}, u32[]{:S(2)}) collective-permute-start(f32[56,768]{1,0:T(8,128)S(1)} %get-tuple-element.86), channel_id=1, source_target_pairs={{0,18},{2,0},{16,2},{18,16},{1,19},{3,1},{17,3},{19,17},{4,22},{6,... | collective-permute-start | bytes 516104 | tf_op jit(solution)/shard_map/ppermute | solution.py:363
  149.2 7.1 %collective-permute-done.27 = f32[56,768]{1,0:T(8,128)S(1)} collective-permute-done((f32[56,768]{1,0:T(8,128)S(1)}, f32[56,768]{1,0:T(8,128)S(1)}, u32[]{:S(2)}, u32[]{:S(2)}) %collective-permute-start.27) | collective-permute-done | bytes 172064 | tf_op jit(solution)/shard_map/ppermute | solution.py:363
  158.4 3.4 %collective-permute-done.30 = f32[56,768]{1,0:T(8,128)S(1)} collective-permute-done((f32[56,768]{1,0:T(8,128)S(1)}, f32[56,768]{1,0:T(8,128)S(1)}, u32[]{:S(2)}, u32[]{:S(2)}) %collective-permute-start.30) | collective-permute-done | bytes 172064 | tf_op jit(solution)/shard_map/ppermute | solution.py:367
  169.2 5.8 %collective-permute-done.32 = f32[56,768]{1,0:T(8,128)S(1)} collective-permute-done((f32[56,768]{1,0:T(8,128)S(1)}, f32[56,768]{1,0:T(8,128)S(1)}, u32[]{:S(2)}, u32[]{:S(2)}) %collective-permute-start.32) | collective-permute-done | bytes 172064 | tf_op jit(solution)/shard_map/ppermute | solution.py:370
  175.0 3.6 %collective-permute-done.33 = f32[56,768]{1,0:T(8,128)S(1)} collective-permute-done((f32[56,768]{1,0:T(8,128)S(1)}, f32[56,768]{1,0:T(8,128)S(1)}, u32[]{:S(2)}, u32[]{:S(2)}) %collective-permute-start.33) | collective-permute-done | bytes 172064 | tf_op jit(solution)/shard_map/ppermute | solution.py:371
  (143 shorter events, 66.2 us)
Async XLA Ops:
  3.6 8.7 %collective-permute-start.7 = (bf16[64,1792]{1,0:T(8,128)(2,1)S(1)}, bf16[64,1792]{1,0:T(8,128)(2,1)S(1)}, u32[]{:S(2)}, u32[]{:S(2)}) collective-permute-start(bf16[64,1792]{1,0:T(8,128)(2,1)S(1)} %pad_maximum_fusion.1), channel_id=1, source_target_pairs={{0,2},{2,16},{16,18},{18,0},{1,3},{3,17},{17,19},{19,1},{4,6},{6,2... | collective-permute-start | bytes 688136 | tf_op jit(solution)/shard_map/ppermute | solution.py:252
  5.3 7.3 %collective-permute-start.8 = (bf16[64,1792]{1,0:T(8,128)(2,1)S(1)}, bf16[64,1792]{1,0:T(8,128)(2,1)S(1)}, u32[]{:S(2)}, u32[]{:S(2)}) collective-permute-start(bf16[64,1792]{1,0:T(8,128)(2,1)S(1)} %pad_maximum_fusion.1), channel_id=1, source_target_pairs={{0,18},{2,0},{16,2},{18,16},{1,19},{3,1},{17,3},{19,17},{4,22},{6,... | collective-permute-start | bytes 688136 | tf_op jit(solution)/shard_map/ppermute | solution.py:253
  12.3 7.8 %collective-permute-start.9 = (bf16[64,1792]{1,0:T(8,128)(2,1)S(1)}, bf16[64,1792]{1,0:T(8,128)(2,1)S(1)}, u32[]{:S(2)}, u32[]{:S(2)}) collective-permute-start(bf16[64,1792]{1,0:T(8,128)(2,1)S(1)} %collective-permute-done.7), channel_id=1, source_target_pairs={{0,2},{2,16},{16,18},{18,0},{1,3},{3,17},{17,19},{19,1},{4,6},{6,2... | collective-permute-start | bytes 688136 | tf_op jit(solution)/shard_map/ppermute | solution.py:254
  21.1 27.2 %collective-permute-start.11 = (bf16[256,1792]{1,0:T(8,128)(2,1)S(1)}, bf16[256,1792]{1,0:T(8,128)(2,1)S(1)}, u32[]{:S(2)}, u32[]{:S(2)}) collective-permute-start(bf16[256,1792]{1,0:T(8,128)(2,1)S(1)} %pad_maximum_fusion.refs_0_), channel_id=1, source_target_pairs={{0,4},{4,8},{8,12},{12,0},{1,5},{5,9},{9,13},{13,1},{2,6},{6,10},{... | collective-permute-start | bytes 2752520 | tf_op jit(solution)/shard_map/ppermute | solution.py:256
  22.6 25.7 %collective-permute-start.13 = (bf16[256,1792]{1,0:T(8,128)(2,1)S(1)}, bf16[256,1792]{1,0:T(8,128)(2,1)S(1)}, u32[]{:S(2)}, u32[]{:S(2)}) collective-permute-start(bf16[256,1792]{1,0:T(8,128)(2,1)S(1)} %pad_maximum_fusion.refs_0_), channel_id=1, source_target_pairs={{0,12},{4,0},{8,4},{12,8},{1,13},{5,1},{9,5},{13,9},{2,14},{6,2},{... | collective-permute-start | bytes 2752520 | tf_op jit(solution)/shard_map/ppermute | solution.py:257
  23.3 9.9 %collective-permute-start = (bf16[64,1792]{1,0:T(8,128)(2,1)S(1)}, bf16[64,1792]{1,0:T(8,128)(2,1)S(1)}, u32[]{:S(2)}, u32[]{:S(2)}) collective-permute-start(bf16[64,1792]{1,0:T(8,128)(2,1)S(1)} %constant_dynamic-update-slice_fusion.refs_0_), channel_id=1, source_target_pairs={{0,32},{32,64},{64,96},{96,128},{128,160},{160,192},{192,224},{224... | collective-permute-start | bytes 688136 | tf_op jit(solution)/shard_map/ppermute | solution.py:246
  25.3 8.6 %collective-permute-start.4 = (bf16[64,1792]{1,0:T(8,128)(2,1)S(1)}, bf16[64,1792]{1,0:T(8,128)(2,1)S(1)}, u32[]{:S(2)}, u32[]{:S(2)}) collective-permute-start(bf16[64,1792]{1,0:T(8,128)(2,1)S(1)} %constant_dynamic-update-slice_fusion.refs_0_), channel_id=1, source_target_pairs={{0,224},{32,0},{64,32},{96,64},{128,96},{160,128},{192,160},{224,1... | collective-permute-start | bytes 688136 | tf_op jit(solution)/shard_map/ppermute | solution.py:248
  33.2 7.8 %collective-permute-start.1 = (bf16[64,1792]{1,0:T(8,128)(2,1)S(1)}, bf16[64,1792]{1,0:T(8,128)(2,1)S(1)}, u32[]{:S(2)}, u32[]{:S(2)}) collective-permute-start(bf16[64,1792]{1,0:T(8,128)(2,1)S(1)} %collective-permute-done.refs_1_), channel_id=1, source_target_pairs={{0,32},{32,64},{64,96},{96,128},{128,160},{160,192},{192,224},{224... | collective-permute-start | bytes 688136 | tf_op jit(solution)/shard_map/ppermute | solution.py:246
  33.9 7.8 %collective-permute-start.5 = (bf16[64,1792]{1,0:T(8,128)(2,1)S(1)}, bf16[64,1792]{1,0:T(8,128)(2,1)S(1)}, u32[]{:S(2)}, u32[]{:S(2)}) collective-permute-start(bf16[64,1792]{1,0:T(8,128)(2,1)S(1)} %collective-permute-done.4.refs_7_), channel_id=1, source_target_pairs={{0,224},{32,0},{64,32},{96,64},{128,96},{160,128},{192,160},{224,1... | collective-permute-start | bytes 688136 | tf_op jit(solution)/shard_map/ppermute | solution.py:248
  41.7 33.8 %collective-permute-start.10 = (bf16[256,1792]{1,0:T(8,128)(2,1)S(1)}, bf16[256,1792]{1,0:T(8,128)(2,1)}, u32[]{:S(2)}, u32[]{:S(2)}) collective-permute-start(bf16[256,1792]{1,0:T(8,128)(2,1)S(1)} %pad_maximum_fusion.refs_0_), channel_id=1, source_target_pairs={{0,1},{1,0},{2,3},{3,2},{4,5},{5,4},{6,7},{7,6},{8,9},{9,8},{10,11... | collective-permute-start | bytes 2752520 | tf_op jit(solution)/shard_map/ppermute | solution.py:251
  41.7 8.8 %collective-permute-start.6 = (bf16[64,1792]{1,0:T(8,128)(2,1)S(1)}, bf16[64,1792]{1,0:T(8,128)(2,1)S(1)}, u32[]{:S(2)}, u32[]{:S(2)}) collective-permute-start(bf16[64,1792]{1,0:T(8,128)(2,1)S(1)} %collective-permute-done.5.refs_6_), channel_id=1, source_target_pairs={{0,224},{32,0},{64,32},{96,64},{128,96},{160,128},{192,160},{224,1... | collective-permute-start | bytes 688136 | tf_op jit(solution)/shard_map/ppermute | solution.py:248
  48.3 32.8 %collective-permute-start.12 = (bf16[256,1792]{1,0:T(8,128)(2,1)S(1)}, bf16[256,1792]{1,0:T(8,128)(2,1)}, u32[]{:S(2)}, u32[]{:S(2)}) collective-permute-start(bf16[256,1792]{1,0:T(8,128)(2,1)S(1)} %collective-permute-done.11.refs_0_), channel_id=1, source_target_pairs={{0,1},{1,0},{2,3},{3,2},{4,5},{5,4},{6,7},{7,6},{8,9},{9,8},{10,11... | collective-permute-start | bytes 2752520 | tf_op jit(solution)/shard_map/ppermute | solution.py:251
  48.4 37.8 %collective-permute-start.14 = (bf16[256,1792]{1,0:T(8,128)(2,1)S(1)}, bf16[256,1792]{1,0:T(8,128)(2,1)}, u32[]{:S(2)}, u32[]{:S(2)}) collective-permute-start(bf16[256,1792]{1,0:T(8,128)(2,1)S(1)} %collective-permute-done.13.refs_0_), channel_id=1, source_target_pairs={{0,1},{1,0},{2,3},{3,2},{4,5},{5,4},{6,7},{7,6},{8,9},{9,8},{10,11... | collective-permute-start | bytes 2752520 | tf_op jit(solution)/shard_map/ppermute | solution.py:251
  51.2 12.1 %collective-permute-start.15 = (bf16[128,1792]{1,0:T(8,128)(2,1)S(1)}, bf16[128,1792]{1,0:T(8,128)(2,1)S(1)}, u32[]{:S(2)}, u32[]{:S(2)}) collective-permute-start(bf16[128,1792]{1,0:T(8,128)(2,1)S(1)} %slice.138), channel_id=1, source_target_pairs={{0,4},{4,8},{8,12},{12,0},{1,5},{5,9},{9,13},{13,1},{2,6},{6,10},{... | collective-permute-start | bytes 1376264 | tf_op jit(solution)/shard_map/ppermute | solution.py:258
  56.2 9.1 %collective-permute-start.16 = (bf16[128,1792]{1,0:T(8,128)(2,1)S(1)}, bf16[128,1792]{1,0:T(8,128)(2,1)}, u32[]{:S(2)}, u32[]{:S(2)}) collective-permute-start(bf16[128,1792]{1,0:T(8,128)(2,1)S(1)} %slice.139), channel_id=1, source_target_pairs={{0,12},{4,0},{8,4},{12,8},{1,13},{5,1},{9,5},{13,9},{2,14},{6,2},{... | collective-permute-start | bytes 1376264 | tf_op jit(solution)/shard_map/ppermute | solution.py:259
  63.3 28.1 %collective-permute-start.17 = (bf16[128,1792]{1,0:T(8,128)(2,1)S(1)}, bf16[128,1792]{1,0:T(8,128)(2,1)}, u32[]{:S(2)}, u32[]{:S(2)}) collective-permute-start(bf16[128,1792]{1,0:T(8,128)(2,1)S(1)} %collective-permute-done.15.refs_0_), channel_id=1, source_target_pairs={{0,1},{1,0},{2,3},{3,2},{4,5},{5,4},{6,7},{7,6},{8,9},{9,8},{10,11... | collective-permute-start | bytes 1376264 | tf_op jit(solution)/shard_map/ppermute | solution.py:251
  65.3 26.1 %collective-permute-start.18 = (bf16[128,1792]{1,0:T(8,128)(2,1)}, bf16[128,1792]{1,0:T(8,128)(2,1)}, u32[]{:S(2)}, u32[]{:S(2)}) collective-permute-start(bf16[128,1792]{1,0:T(8,128)(2,1)} %collective-permute-done.16.refs_1_), channel_id=1, source_target_pairs={{0,1},{1,0},{2,3},{3,2},{4,5},{5,4},{6,7},{7,6},{8,9},{9,8},{10,11... | collective-permute-start | bytes 1376264 | tf_op jit(solution)/shard_map/ppermute | solution.py:251
  106.9 19.6 %collective-permute-start.21 = (f32[5,512]{1,0:T(8,128)S(1)}, f32[5,512]{1,0:T(8,128)S(1)}, u32[]{:S(2)}, u32[]{:S(2)}) collective-permute-start(f32[5,512]{1,0:T(8,128)S(1)} %stack.21), channel_id=1, source_target_pairs={{0,160},{32,192},{64,224},{96,0},{128,32},{160,64},{192,96},{224,1... | collective-permute-start | bytes 30728 | tf_op jit(solution)/shard_map/ppermute | solution.py:318
  109.1 17.4 %collective-permute-start.22 = (f32[5,512]{1,0:T(8,128)S(1)}, f32[5,512]{1,0:T(8,128)S(1)}, u32[]{:S(2)}, u32[]{:S(2)}) collective-permute-start(f32[5,512]{1,0:T(8,128)S(1)} %stack.22), channel_id=1, source_target_pairs={{0,96},{32,128},{64,160},{96,192},{128,224},{160,0},{192,32},{224,... | collective-permute-start | bytes 30728 | tf_op jit(solution)/shard_map/ppermute | solution.py:319
  134.5 10.7 %collective-permute-start.26 = (bf16[112,768]{1,0:T(8,128)(2,1)S(1)}, bf16[112,768]{1,0:T(8,128)(2,1)S(1)}, u32[]{:S(2)}, u32[]{:S(2)}) collective-permute-start(bf16[112,768]{1,0:T(8,128)(2,1)S(1)} %get-tuple-element.84), channel_id=1, source_target_pairs={{0,8},{4,12},{8,0},{12,4},{1,9},{5,13},{9,1},{13,5},{2,10},{6,14},... | collective-permute-start | bytes 516104 | tf_op jit(solution)/shard_map/ppermute | solution.py:353
  145.9 10.4 %collective-permute-start.27 = (f32[56,768]{1,0:T(8,128)S(1)}, f32[56,768]{1,0:T(8,128)S(1)}, u32[]{:S(2)}, u32[]{:S(2)}) collective-permute-start(f32[56,768]{1,0:T(8,128)S(1)} %get-tuple-element.86), channel_id=1, source_target_pairs={{0,2},{2,16},{16,18},{18,0},{1,3},{3,17},{17,19},{19,1},{4,6},{6,2... | collective-permute-start | bytes 516104 | tf_op jit(solution)/shard_map/ppermute | solution.py:363
  146.0 10.3 %collective-permute-start.28 = (f32[56,768]{1,0:T(8,128)S(1)}, f32[56,768]{1,0:T(8,128)S(1)}, u32[]{:S(2)}, u32[]{:S(2)}) collective-permute-start(f32[56,768]{1,0:T(8,128)S(1)} %get-tuple-element.86), channel_id=1, source_target_pairs={{0,18},{2,0},{16,2},{18,16},{1,19},{3,1},{17,3},{19,17},{4,22},{6,... | collective-permute-start | bytes 516104 | tf_op jit(solution)/shard_map/ppermute | solution.py:363
  164.7 10.3 %collective-permute-start.32 = (f32[56,768]{1,0:T(8,128)S(1)}, f32[56,768]{1,0:T(8,128)S(1)}, u32[]{:S(2)}, u32[]{:S(2)}) collective-permute-start(f32[56,768]{1,0:T(8,128)S(1)} %get-tuple-element.87), channel_id=1, source_target_pairs={{0,160},{32,192},{64,224},{96,0},{128,32},{160,64},{192,96},{224,1... | collective-permute-start | bytes 516104 | tf_op jit(solution)/shard_map/ppermute | solution.py:370
  167.4 11.2 %collective-permute-start.33 = (f32[56,768]{1,0:T(8,128)S(1)}, f32[56,768]{1,0:T(8,128)S(1)}, u32[]{:S(2)}, u32[]{:S(2)}) collective-permute-start(f32[56,768]{1,0:T(8,128)S(1)} %get-tuple-element.88), channel_id=1, source_target_pairs={{0,96},{32,128},{64,160},{96,192},{128,224},{160,0},{192,32},{224,... | collective-permute-start | bytes 516104 | tf_op jit(solution)/shard_map/ppermute | solution.py:371
  (42 other events, 230.2 us)
